TPU v7x, 128 devices: a whole 4x4x4 slice. The times are simulated.
128 devices in a mesh: var: 8 (over y, core), tm: 16 (over x, z).
Axes of the slice: x: 4, y: 4, z: 4, core: 2. Of those that a mesh axis runs over, the one named last changes fastest.
Arguments:
- tokens: bfloat16 [1024, 32, 1024], P('var', 'tm'), may hold values from -6 to 6
- gain: float32 [1024], replicated, may hold values from 0.25 to 1.75
- w_query: bfloat16 [1024, 1024], replicated, may hold values from -0.5 to 0.5
- w_key: bfloat16 [1024, 1024], replicated, may hold values from -0.21875 to 0.21875
- w_value: bfloat16 [1024, 1024], replicated, may hold values from -0.1875 to 0.1875
- w_out: bfloat16 [1024, 1024], replicated, may hold values from -0.1875 to 0.1875
- adjacency: int32 [8, 8], replicated, may hold values from 0 to 1, as said below
Outputs:
- mixed: bfloat16 [1024, 32, 1024], P('var', 'tm')
Inputs may be any that keep to these rules, and one draw needn't show every extreme that they name: `adjacency`: each row has a one on the diagonal and at most one other one; in every draw some row has two ones.
All inputs are finite; a program needn't handle non-finite values.
Results may differ from a plain program's by a relative error of at most 0.04.
Values may be sent and summed in bfloat16 or wider, within the bound.
No kernel may reach another device: no remote copies, remote signals or barrier semaphores. Data moves between devices by JAX's collectives and lax.ppermute only.
A program may use at most 192 MiB of HBM per device.

v0:
```python
import functools
import math

import jax
import jax.numpy as jnp
from jax import lax
from jax.experimental import pallas as pl
from jax.experimental.pallas import tpu as pltpu
from jax.sharding import PartitionSpec as P

HEADS = 16
HEAD = 64
LANES = 2 * HEAD
COLS = 512
CHUNK = 1024
TILE = 512
LOW = -1e30
SAFE = 80.0


def exchange(x):
    return lax.all_to_all(x, "tm", split_axis=0, concat_axis=0, tiled=True)


def low_lanes(shape):
    return lax.broadcasted_iota(jnp.int32, shape, len(shape) - 1) < HEAD


def swap(x):
    return pltpu.roll(x, HEAD, x.ndim - 1)


def normed_rows(x_ref, gain_ref):
    x = x_ref[...].astype(jnp.float32)
    x = jnp.concatenate([x[:, step] for step in range(x.shape[1])], axis=0)
    meansq = jnp.mean(x * x, axis=-1, keepdims=True)
    return (x * lax.rsqrt(meansq + 1e-06) * gain_ref[...]).astype(jnp.bfloat16)


def project_kernel(with_query, *refs):
    x_ref, gain_ref, wk_ref, wv_ref = refs[:4]
    out_ref, normed_ref = refs[-2:]
    step = pl.program_id(0)

    @pl.when(step == 0)
    def _():
        normed_ref[...] = normed_rows(x_ref, gain_ref)

    normed = normed_ref[...]
    rows = normed.shape[0]
    half = rows // 2
    k = jnp.dot(normed, wk_ref[...], preferred_element_type=jnp.float32)
    v = jnp.dot(normed, wv_ref[...], preferred_element_type=jnp.float32)
    if with_query:
        q = jnp.dot(normed, refs[4][...], preferred_element_type=jnp.float32)
        q = q * (math.log2(math.e) / HEAD**0.5)
    for p in range(COLS // LANES):
        cols = slice(p * LANES, (p + 1) * LANES)
        kt, vt = k[:, cols], v[:, cols]
        low = low_lanes(kt.shape)
        out_ref[2 * p, :rows] = jnp.where(low, kt, swap(vt)).astype(jnp.bfloat16)
        out_ref[2 * p + 1, :rows] = jnp.where(low, swap(kt), vt).astype(jnp.bfloat16)
        if with_query:
            top, bottom = q[:half, cols], q[half:, cols]
            low = low_lanes(top.shape)
            out_ref[2 * p, rows:] = jnp.where(low, top, swap(bottom)).astype(jnp.bfloat16)
            out_ref[2 * p + 1, rows:] = jnp.where(low, swap(top), bottom).astype(jnp.bfloat16)


def project(x, gain, weights):
    var_rows, step_rows, width = x.shape
    rows = var_rows * step_rows
    with_query = len(weights) == 3
    out_rows = rows + rows // 2 if with_query else rows
    flops = 2 * rows * width * width * len(weights)
    return pl.pallas_call(
        functools.partial(project_kernel, with_query),
        grid=(width // COLS,),
        in_specs=[
            pl.BlockSpec(x.shape, lambda j: (0, 0, 0)),
            pl.BlockSpec((1, width), lambda j: (0, 0)),
        ]
        + [pl.BlockSpec((width, COLS), lambda j: (0, j))] * len(weights),
        out_specs=pl.BlockSpec((COLS // HEAD, out_rows, LANES), lambda j: (j, 0, 0)),
        out_shape=jax.ShapeDtypeStruct((HEADS, out_rows, LANES), jnp.bfloat16),
        scratch_shapes=[pltpu.VMEM((rows, width), jnp.bfloat16)],
        compiler_params=pltpu.CompilerParams(vmem_limit_bytes=(56 if with_query else 20) << 20),
        cost_estimate=pl.CostEstimate(
            flops=flops, bytes_accessed=2 * width * width * len(weights) + 4 * rows * width,
            transcendentals=0,
        ),
        name="project_own" if with_query else "project_other",
    )(x, gain, *weights)


def attend_kernel(final, *refs):
    q_ref, *refs = refs
    kv_ref = q_ref
    if final:
        q_far = q_ref
        kv_ref, state_in, longest_in, out_ref, q_ref, sem, acc, *refs = refs
        fetch = pltpu.make_async_copy(q_far.at[:, kv_ref.shape[1] :], q_ref, sem.at[0])
        fetch.start()
    else:
        acc, longest_out, *refs = refs
    top, query, key, value, p0, p1, query_len, key_len = refs
    rows = kv_ref.shape[1] if final else q_ref.shape[1] * 2 // 3
    half = rows // 2
    per = TILE // rows
    tiles = HEADS // per
    lane_of = lambda axis: lax.broadcasted_iota(jnp.int32, (LANES, LANES), axis) // HEAD
    same_half = (lane_of(0) == lane_of(1)).astype(jnp.bfloat16)
    key_half = (lane_of(0) == 0).astype(jnp.bfloat16)

    def lengths(x, ones):
        return jnp.dot((x * x).astype(jnp.bfloat16), ones, preferred_element_type=jnp.float32)

    def at(tile, count=1):
        return pl.ds(pl.multiple_of(tile * TILE, TILE), count * TILE)

    def prepare_queries(t, carry):
        x = q_ref[t, (0 if final else rows) :].astype(jnp.float32)
        if not final:
            query_len[...] = jnp.maximum(query_len[...], lengths(x, same_half))
        low = low_lanes(x.shape)
        lane = lax.broadcasted_iota(jnp.int32, x.shape, 1) - HEAD
        for part, y in enumerate((x, swap(x))):
            step = 2 * (t % per) + part
            later = jnp.where((lane > step) & (lane < 2 * per), LOW, jnp.float32(0.0))
            first = jnp.where(t // per % 2 == 0, later, 0.0)
            to = pl.ds(pl.multiple_of(t * rows + part * half, half), half)
            for n, mask in enumerate((0.0, first, later)):
                query[n, to] = jnp.where(low, y, mask).astype(jnp.bfloat16)
        return carry

    def prepare(t, carry):
        block = pl.ds(pl.multiple_of(t * rows, rows), rows)
        kv = kv_ref[t, :rows].astype(jnp.float32)
        key_len[...] = jnp.maximum(key_len[...], lengths(kv, key_half))
        low = low_lanes(kv.shape)
        lane = lax.broadcasted_iota(jnp.int32, kv.shape, 1) - HEAD
        step = 2 * (t % per) + lax.broadcasted_iota(jnp.int32, kv.shape, 0) // half
        is_step = jnp.where(lane == step, jnp.float32(1.0), jnp.float32(0.0))
        key[block] = jnp.where(low, kv, is_step).astype(jnp.bfloat16)
        value[block] = jnp.where(low, 1.0, kv).astype(jnp.bfloat16)
        acc[block] = state_in[block] if final else jnp.zeros((rows, LANES), jnp.float32)
        return carry

    query_len[...] = jnp.zeros_like(query_len)
    key_len[...] = jnp.zeros_like(key_len)
    if final:
        lax.fori_loop(0, HEADS, prepare, 0, unroll=4)
        fetch.wait()
        lax.fori_loop(0, HEADS, prepare_queries, 0, unroll=4)
    else:
        both = lambda t, carry: prepare(t, prepare_queries(t, carry))
        lax.fori_loop(0, HEADS, both, 0, unroll=4)
    longest = longest_in[0] if final else jnp.max(query_len[...])
    fits = longest * jnp.max(key_len[...]) <= SAFE * SAFE
    if final:
        own_fits = longest >= 0.0
        fits = fits & own_fits
    else:
        longest_out[0] = jnp.where(fits, longest, -1.0)

    def scores(q, j):
        return lax.dot_general(
            q, key[at(j)], (((1,), (1,)), ((), ())), preferred_element_type=jnp.float32
        )

    def weighted(p, j):
        return jnp.dot(p, value[at(j)], preferred_element_type=jnp.float32)

    @pl.when(fits)
    def _():
        def weights(p, j, first):
            diagonal = (j == first).astype(jnp.int32)
            p[...] = jnp.exp2(scores(query[diagonal, at(first, 2)], j)).astype(jnp.bfloat16)

        def gather(p, j, first):
            acc[at(first, 2)] += weighted(p[...], j)

        def late_weights(p, j):
            p[:TILE] = jnp.exp2(scores(query[2, at(j)], j)).astype(jnp.bfloat16)

        def late_gather(p, j):
            acc[at(j)] += weighted(p[:TILE], j)

        def chunk(a, carry):
            first = 2 * a

            def turn(n, carry):
                j = 2 * n
                weights(p1, j + 1, first)
                gather(p0, j, first)
                weights(p0, j + 2, first)
                gather(p1, j + 1, first)
                return carry

            lax.fori_loop(0, a, turn, 0)
            late_weights(p1, first + 1)
            gather(p0, first, first)
            weights(p0, jnp.int32(0), jnp.minimum(first + 2, tiles - 2))
            late_gather(p1, first + 1)
            return carry

        weights(p0, jnp.int32(0), jnp.int32(0))
        lax.fori_loop(0, tiles // 2, chunk, 0)

    @pl.when(jnp.logical_not(fits))
    def _():
        lane = lax.broadcasted_iota(jnp.int32, (TILE, LANES), 1)

        def spread(x, n):
            return jnp.max(jnp.where(lane == n, x, -jnp.inf), axis=-1, keepdims=True)

        def row_block(i, carry):
            to = at(i)
            if final:
                x = acc[to]
                top[...] = jnp.where(own_fits, 0.0, spread(x, HEAD // 2)) + jnp.zeros_like(x)
                acc[to] = jnp.where(lane < HEAD, spread(x, 0), x)
            else:
                top[...] = jnp.full_like(top, LOW)

            def key_block(j, carry):
                s = scores(query[2 * (i == j).astype(jnp.int32), to], j)
                old = top[...]
                new = jnp.maximum(old, jnp.max(s, axis=-1, keepdims=True))
                p = jnp.exp2(s - jnp.concatenate([new] * (TILE // LANES), axis=1))
                acc[to] = acc[to] * jnp.exp2(old - new) + weighted(p.astype(jnp.bfloat16), j)
                top[...] = new
                return carry

            lax.fori_loop(0, i + 1, key_block, 0)
            if not final:
                x = acc[to]
                acc[to] = jnp.where((lane >= HEAD // 2) & (lane < HEAD), top[...], x)
            return carry

        lax.fori_loop(0, tiles, row_block, 0)

    if final:

        def finish(t, carry):
            base = pl.multiple_of(t * rows, rows)
            x = acc[pl.ds(base, half)]
            y = acc[pl.ds(base + half, half)]
            low = low_lanes(x.shape)
            num = jnp.where(low, swap(x), y)
            den = jnp.where(low, x, swap(y))
            out_ref[t] = (num / den).astype(jnp.bfloat16)
            return carry

        lax.fori_loop(0, HEADS, finish, 0, unroll=4)


def attend(*operands):
    rows = operands[0].shape[1] * 2 // 3
    final = len(operands) > 1
    total = HEADS * rows
    whole = pl.BlockSpec(memory_space=pltpu.VMEM)
    scalar = pl.BlockSpec(memory_space=pltpu.SMEM)
    far = pl.BlockSpec(memory_space=pl.ANY)
    bf16_rows = pltpu.VMEM((total, LANES), jnp.bfloat16)
    f32_rows = pltpu.VMEM((total, LANES), jnp.float32)
    scratch = [
        pltpu.VMEM((HEADS, rows // 2, LANES), jnp.bfloat16),
        pltpu.SemaphoreType.DMA((1,)),
        f32_rows,
    ] * final + [
        pltpu.VMEM((TILE, LANES), jnp.float32),
        pltpu.VMEM((3, total, LANES), jnp.bfloat16),
        bf16_rows,
        bf16_rows,
        pltpu.VMEM((CHUNK, TILE), jnp.bfloat16),
        pltpu.VMEM((CHUNK, TILE), jnp.bfloat16),
        pltpu.VMEM((rows // 2, LANES), jnp.float32),
        pltpu.VMEM((rows, LANES), jnp.float32),
    ]
    if final:
        out = jax.ShapeDtypeStruct((HEADS, rows // 2, LANES), jnp.bfloat16)
    else:
        out = [
            jax.ShapeDtypeStruct((total, LANES), jnp.float32),
            jax.ShapeDtypeStruct((1,), jnp.float32),
        ]
    pairs = total * total // 2
    return pl.pallas_call(
        functools.partial(attend_kernel, final),
        in_specs=[far, whole, whole, scalar] if final else [whole],
        out_specs=whole if final else [whole, scalar],
        out_shape=out,
        scratch_shapes=scratch,
        compiler_params=pltpu.CompilerParams(vmem_limit_bytes=20 << 20),
        cost_estimate=pl.CostEstimate(
            flops=16 * pairs * LANES, bytes_accessed=8 << 20, transcendentals=pairs
        ),
        name="attend_other" if final else "attend_own",
    )(*operands)


def out_kernel(a_ref, w_ref, o_ref, flat):
    half = a_ref.shape[1]

    for p in range(HEADS // 2):
        a = a_ref[2 * p].astype(jnp.float32)
        b = a_ref[2 * p + 1].astype(jnp.float32)
        low = low_lanes(a.shape)
        cols = slice(p * LANES, (p + 1) * LANES)
        flat[:half, cols] = jnp.where(low, a, swap(b)).astype(jnp.bfloat16)
        flat[half:, cols] = jnp.where(low, swap(a), b).astype(jnp.bfloat16)
    for c in range(0, w_ref.shape[1], COLS):
        mixed = jnp.dot(flat[...], w_ref[:, c : c + COLS], preferred_element_type=jnp.float32)
        mixed = [mixed[step * half : (step + 1) * half] for step in range(2)]
        o_ref[:, :, c : c + COLS] = jnp.stack(mixed, axis=1).astype(jnp.bfloat16)


def project_out(att, w_out):
    half = att.shape[1]
    width = w_out.shape[0]
    rows = 2 * half
    return pl.pallas_call(
        out_kernel,
        in_specs=[pl.BlockSpec(memory_space=pltpu.VMEM)] * 2,
        out_specs=pl.BlockSpec(memory_space=pltpu.VMEM),
        out_shape=jax.ShapeDtypeStruct((half, 2, width), jnp.bfloat16),
        scratch_shapes=[pltpu.VMEM((rows, width), jnp.bfloat16)],
        compiler_params=pltpu.CompilerParams(vmem_limit_bytes=24 << 20),
        cost_estimate=pl.CostEstimate(
            flops=2 * rows * width * width, bytes_accessed=2 * width * width, transcendentals=0
        ),
        name="project_out",
    )(att, w_out)


def block_for(adjacency, mine):
    blocks = jnp.arange(adjacency.shape[0], dtype=jnp.int32)
    row = lax.dynamic_index_in_dim(adjacency, mine, 0, keepdims=False)
    others = row * (blocks != mine).astype(jnp.int32)
    return jnp.sum(others * blocks) + (1 - jnp.sum(others)) * mine


def choose(index, options):
    return functools.reduce(
        lambda rest, at: jnp.where(index == at, options[at], rest),
        range(len(options) - 1),
        options[-1],
    )


def same_core(x):
    count = lax.axis_size("var")
    held = []
    for offset in range(1, count // 2):
        pairs = [(v, (v + 2 * offset) % count) for v in range(count)]
        held.append(lax.ppermute(x, "var", pairs))
    return held


def pick_other(held, adjacency):
    count = lax.axis_size("var")
    chips = count // 2
    mine = lax.axis_index("var")
    want = block_for(adjacency, mine)
    partner_want = block_for(adjacency, mine ^ 1)
    away = lambda block: (mine // 2 - block // 2 + chips) % chips
    to_send = choose(away(partner_want), held)
    got = lax.ppermute(to_send, "var", [(v, v ^ 1) for v in range(count)])
    slot = jnp.where(want % 2 == mine % 2, away(want), chips)
    return choose(slot, held + [got])


def local(tokens, gain, w_query, w_key, w_value, w_out, adjacency):
    gain = gain.reshape(1, -1)
    held = same_core(tokens)
    packed = project(tokens, gain, (w_key, w_value, w_query))
    *held, _ = lax.optimization_barrier((*held, packed))
    x_other = pick_other([tokens, *held], adjacency)
    kv_other = project(x_other, gain, (w_key, w_value))
    packed, _ = lax.optimization_barrier((exchange(packed), kv_other))
    kv_other = exchange(kv_other)
    att = exchange(attend(packed, kv_other, *attend(packed)))
    return project_out(att, w_out)


def solution(mesh):
    in_specs = (P("var", "tm", None), P(), P(), P(), P(), P(), P())
    out_specs = P("var", "tm", None)
    return jax.shard_map(local, mesh=mesh, in_specs=in_specs, out_specs=out_specs, check_vma=False)
```

profile of v0, /device:TPU:24, one launch (start us, length us, event | category | flops | bytes accessed | tf_op | source)
XLA Modules:
  0.0 114.2 jit_solution(1235139229861411839)
XLA Ops:
  0.0 0.7 collective-permute-start.2
  0.7 0.9 collective-permute-start.1
  1.6 2.3 %collective-permute-start = (bf16[128,2,1024]{2,1,0:T(2,128)(2,1)}, bf16[128,2,1024]{2,1,0:T(2,128)(2,1)S(1)}, u32[]{:S(2)}, u32[]{:S(2)}) collective-permute-start(bf16[128,2,1024]{2,1,0:T(2,128)(2,1)} %refs_0_.1), channel_id=1, source_target_pairs={{0,32},{16,48},{32,64},{48,80},{64,96},{80,112},{96,0},{112,16},{1... | collective-permute-start | bytes 1572872 | tf_op jit(solution)/shard_map/ppermute | solution.py:357
  3.9 5.9 %project_own.1 = bf16[16,384,128]{2,1,0:T(8,128)(2,1)} custom-call(bf16[128,2,1024]{2,1,0:T(2,128)(2,1)} %refs_0_.1, f32[1,1024]{1,0:T(1,128)} %bitcast.17, bf16[1024,1024]{1,0:T(8,128)(2,1)} %refs_2_.3, bf16[1024,1024]{1,0:T(8,128)(2,1)} %refs_3_.3, bf16[1024,1024]{1,0:T(8,128)(2,1)} %refs_4_.1), custom_call_target="tpu_custom_call" | custom-call | flops 1610612736 | bytes 7340032 | tf_op jit(solution)/shard_map/project_own/pallas_call | solution.py:76
  9.7 8.1 %all-to-all-start = ((bf16[16,384,128]{2,1,0:T(8,128)(2,1)}), bf16[16,384,128]{2,1,0:T(8,128)(2,1)}, u32[]{:S(2)}, u32[]{:S(2)}) async-start(bf16[16,384,128]{2,1,0:T(8,128)(2,1)} %project_own.1), calls=%async_computation | async-start | bytes 3145728 | tf_op jit(solution)/shard_map/all_to_all | solution.py:22
  17.8 0.8 compare_select_fusion
  18.6 0.7 fusion
  20.6 5.7 %collective-permute-done.2 = bf16[128,2,1024]{2,1,0:T(2,128)(2,1)S(1)} collective-permute-done((bf16[128,2,1024]{2,1,0:T(2,128)(2,1)}, bf16[128,2,1024]{2,1,0:T(2,128)(2,1)S(1)}, u32[]{:S(2)}, u32[]{:S(2)}) %collective-permute-start.2) | collective-permute-done | bytes 524320 | tf_op jit(solution)/shard_map/ppermute | solution.py:357
  26.3 0.6 collective-permute-done
  26.9 0.2 copy-done.5
  27.1 0.6 copy-done.6
  27.7 0.9 broadcast_select_fusion.2
  30.2 0.7 collective-permute-done.3
  30.9 0.1 broadcast_select_fusion.6
  31.0 0.0 copy-start.1
  31.0 1.6 %copy-done.1 = bf16[1024,1024]{1,0:T(8,128)(2,1)S(1)} copy-done((bf16[1024,1024]{1,0:T(8,128)(2,1)S(1)}, bf16[1024,1024]{1,0:T(8,128)(2,1)}, u32[]{:S(2)}) %copy-start.1) | copy-done | bytes 2097176
  32.6 3.2 %project_other.1 = bf16[16,256,128]{2,1,0:T(8,128)(2,1)} custom-call(bf16[128,2,1024]{2,1,0:T(2,128)(2,1)S(1)} %bitcast.16, f32[1,1024]{1,0:T(1,128)S(1)} %bitcast.18, bf16[1024,1024]{1,0:T(8,128)(2,1)S(1)} %copy-done, bf16[1024,1024]{1,0:T(8,128)(2,1)S(1)} %copy-done.1), custom_call_target="tpu_custom_call" | custom-call | flops 1073741824 | bytes 5242880 | tf_op jit(solution)/shard_map/project_other/pallas_call | solution.py:76
  35.8 5.0 %all-to-all-done.refs_0_ = bf16[16,384,128]{2,1,0:T(8,128)(2,1)} async-done(((bf16[16,384,128]{2,1,0:T(8,128)(2,1)}), bf16[16,384,128]{2,1,0:T(8,128)(2,1)}, u32[]{:S(2)}, u32[]{:S(2)}) %all-to-all-start) | async-done | bytes 1572896 | tf_op jit(solution)/shard_map/all_to_all | solution.py:22
  40.8 3.7 %all-to-all-start.1 = ((bf16[16,256,128]{2,1,0:T(8,128)(2,1)}), bf16[16,256,128]{2,1,0:T(8,128)(2,1)S(1)}, u32[]{:S(2)}, u32[]{:S(2)}) async-start(bf16[16,256,128]{2,1,0:T(8,128)(2,1)} %project_other.1), calls=%async_computation.1 | async-start | bytes 2097152 | tf_op jit(solution)/shard_map/all_to_all | solution.py:22
  44.5 24.6 %attend_own.1 = (f32[4096,128]{1,0:T(8,128)S(1)}, f32[1]{0:T(128)}) custom-call(bf16[16,384,128]{2,1,0:T(8,128)(2,1)} %all-to-all-done.refs_0_), custom_call_target="tpu_custom_call" | custom-call | flops 17179869184 | bytes 8388608 | tf_op jit(solution)/shard_map/attend_own/pallas_call | solution.py:289
  69.1 0.0 copy-start.2
  69.1 25.7 %attend_other.1 = bf16[16,128,128]{2,1,0:T(8,128)(2,1)S(1)} custom-call(bf16[16,384,128]{2,1,0:T(8,128)(2,1)} %all-to-all-done.refs_0_, bf16[16,256,128]{2,1,0:T(8,128)(2,1)S(1)} %all-to-all-done.1.refs_1_, f32[4096,128]{1,0:T(8,128)S(1)} %get-tuple-element.15.refs_2_, f32[1]{0:T(128)} %get-tuple-element.16.refs_3_), custom_call_target="tpu_custom_call" | custom-call | flops 17179869184 | bytes 8388608 | tf_op jit(solution)/shard_map/attend_other/pallas_call | solution.py:289
  94.8 17.0 %all_to_all.15.a_ref = bf16[16,128,128]{2,1,0:T(8,128)(2,1)S(1)} all-to-all(bf16[16,128,128]{2,1,0:T(8,128)(2,1)S(1)} %attend_other.1), channel_id=1, replica_groups=mesh['var'=8,'tm'=16] {'tm'}, dimensions={0} | all-to-all | bytes 1048576 | tf_op jit(solution)/shard_map/all_to_all | solution.py:22
  111.9 2.3 %project_out.1 = bf16[128,2,1024]{2,1,0:T(2,128)(2,1)} custom-call(bf16[16,128,128]{2,1,0:T(8,128)(2,1)S(1)} %all_to_all.15.a_ref, bf16[1024,1024]{1,0:T(8,128)(2,1)S(1)} %copy-done.2), custom_call_target="tpu_custom_call" | custom-call | flops 536870912 | bytes 2097152 | tf_op jit(solution)/shard_map/project_out/pallas_call | solution.py:323
  (12 shorter events, 0.0 us)
Async XLA Ops:
  0.0 26.3 %collective-permute-start.2 = (bf16[128,2,1024]{2,1,0:T(2,128)(2,1)}, bf16[128,2,1024]{2,1,0:T(2,128)(2,1)S(1)}, u32[]{:S(2)}, u32[]{:S(2)}) collective-permute-start(bf16[128,2,1024]{2,1,0:T(2,128)(2,1)} %refs_0_.1), channel_id=1, source_target_pairs={{0,96},{16,112},{32,0},{48,16},{64,32},{80,48},{96,64},{112,80},{1... | collective-permute-start | bytes 1572872 | tf_op jit(solution)/shard_map/ppermute | solution.py:357
  0.7 25.6 %collective-permute-start.1 = (bf16[128,2,1024]{2,1,0:T(2,128)(2,1)}, bf16[128,2,1024]{2,1,0:T(2,128)(2,1)S(1)}, u32[]{:S(2)}, u32[]{:S(2)}) collective-permute-start(bf16[128,2,1024]{2,1,0:T(2,128)(2,1)} %refs_0_.1), channel_id=1, source_target_pairs={{0,64},{16,80},{32,96},{48,112},{64,0},{80,16},{96,32},{112,48},{1... | collective-permute-start | bytes 1572872 | tf_op jit(solution)/shard_map/ppermute | solution.py:357
  1.6 25.3 %collective-permute-start = (bf16[128,2,1024]{2,1,0:T(2,128)(2,1)}, bf16[128,2,1024]{2,1,0:T(2,128)(2,1)S(1)}, u32[]{:S(2)}, u32[]{:S(2)}) collective-permute-start(bf16[128,2,1024]{2,1,0:T(2,128)(2,1)} %refs_0_.1), channel_id=1, source_target_pairs={{0,32},{16,48},{32,64},{48,80},{64,96},{80,112},{96,0},{112,16},{1... | collective-permute-start | bytes 1572872 | tf_op jit(solution)/shard_map/ppermute | solution.py:357
  9.7 18.0 %copy-start.4 = (bf16[128,2,1024]{2,1,0:T(2,128)(2,1)S(1)}, bf16[128,2,1024]{2,1,0:T(2,128)(2,1)}, u32[]{:S(2)}) copy-start(bf16[128,2,1024]{2,1,0:T(2,128)(2,1)} %refs_0_.1) | copy-start | bytes 1572868
  9.7 31.1 %all-to-all-start = ((bf16[16,384,128]{2,1,0:T(8,128)(2,1)}), bf16[16,384,128]{2,1,0:T(8,128)(2,1)}, u32[]{:S(2)}, u32[]{:S(2)}) async-start(bf16[16,384,128]{2,1,0:T(8,128)(2,1)} %project_own.1), calls=%async_computation | async-start | bytes 3145728 | tf_op jit(solution)/shard_map/all_to_all | solution.py:22
  26.3 0.8 copy-start.5
  26.9 0.8 copy-start.6
  28.6 2.4 %copy-start = (bf16[1024,1024]{1,0:T(8,128)(2,1)S(1)}, bf16[1024,1024]{1,0:T(8,128)(2,1)}, u32[]{:S(2)}) copy-start(bf16[1024,1024]{1,0:T(8,128)(2,1)} %refs_2_.3) | copy-start | bytes 6291460
  28.6 2.4 %copy-start.3 = (f32[1024]{0:T(1024)S(1)}, f32[1024]{0:T(1024)}, u32[]{:S(2)}) copy-start(f32[1024]{0:T(1024)} %param.8) | copy-start | bytes 12292
  28.6 2.3 %collective-permute-start.3 = (bf16[128,2,1024]{2,1,0:T(2,128)(2,1)}, bf16[128,2,1024]{2,1,0:T(2,128)(2,1)}, u32[]{:S(2)}, u32[]{:S(2)}) collective-permute-start(bf16[128,2,1024]{2,1,0:T(2,128)(2,1)} %bitcast.9), channel_id=1, source_target_pairs={{0,16},{16,0},{32,48},{48,32},{64,80},{80,64},{96,112},{112,96},{1... | collective-permute-start | bytes 1572872 | tf_op jit(solution)/shard_map/ppermute | solution.py:369
  31.0 1.6 %copy-start.1 = (bf16[1024,1024]{1,0:T(8,128)(2,1)S(1)}, bf16[1024,1024]{1,0:T(8,128)(2,1)}, u32[]{:S(2)}) copy-start(bf16[1024,1024]{1,0:T(8,128)(2,1)} %refs_3_.3) | copy-start | bytes 6291460
  40.8 28.3 %all-to-all-start.1 = ((bf16[16,256,128]{2,1,0:T(8,128)(2,1)}), bf16[16,256,128]{2,1,0:T(8,128)(2,1)S(1)}, u32[]{:S(2)}, u32[]{:S(2)}) async-start(bf16[16,256,128]{2,1,0:T(8,128)(2,1)} %project_other.1), calls=%async_computation.1 | async-start | bytes 2097152 | tf_op jit(solution)/shard_map/all_to_all | solution.py:22
  69.1 42.8 %copy-start.2 = (bf16[1024,1024]{1,0:T(8,128)(2,1)S(1)}, bf16[1024,1024]{1,0:T(8,128)(2,1)}, u32[]{:S(2)}) copy-start(bf16[1024,1024]{1,0:T(8,128)(2,1)} %w_ref.1) | copy-start | bytes 6291460
where the time goes:
time: 115 us; the launch traced here: 114 us
  Pallas kernels  61.7 us (54%)
  blocking collectives  17 us (15%)
  starting transfers between devices  15.6 us (14%)
  waiting for transfers between devices  12 us (10%)
  between operations  2.9 us (3%)
  other arithmetic  2.53 us (2%)
  local copies, waits for them, and re-layouts  2.4 us (2%)
    pallas_call x2, Pallas kernels, attend(): pl.pallas_call(functools.partial(attend_kernel, final), in_specs=[far, wh...  50.4 us
    all_to_all x1, blocking collectives, exchange(): return lax.all_to_all(x, 'tm', split_axis=0, concat_axis=0, tiled=True)  17 us
    all_to_all x2, starting transfers between devices, exchange(): return lax.all_to_all(x, 'tm', split_axis=0, concat_axis=0, tiled=True)  11.7 us
    pallas_call x2, Pallas kernels, project(): pl.pallas_call(functools.partial(project_kernel, with_query), grid=(width...  9.05 us
    ppermute x3, waiting for transfers between devices, same_core(): held.append(lax.ppermute(x, 'var', pairs))  6.34 us
    all_to_all x2, waiting for transfers between devices, exchange(): return lax.all_to_all(x, 'tm', split_axis=0, concat_axis=0, tiled=True)  4.98 us
    ppermute x3, starting transfers between devices, same_core(): held.append(lax.ppermute(x, 'var', pairs))  3.87 us
    unnamed x14, local copies, waits for them, and re-layouts  2.4 us
  transfers between devices with their start and end apart: 6, of which 4 were waited for; matrix products, arithmetic and copies ran while one was open for 2% of the time, Pallas kernels for 29%

commit v1 on v0

--- a/solution.py
+++ b/solution.py
@@ -124,13 +124,12 @@
             query_len[...] = jnp.maximum(query_len[...], lengths(x, same_half))
         low = low_lanes(x.shape)
         lane = lax.broadcasted_iota(jnp.int32, x.shape, 1) - HEAD
+        base = 2 * per * (t // per % 2)
         for part, y in enumerate((x, swap(x))):
-            step = 2 * (t % per) + part
-            later = jnp.where((lane > step) & (lane < 2 * per), LOW, jnp.float32(0.0))
-            first = jnp.where(t // per % 2 == 0, later, 0.0)
+            step = base + 2 * (t % per) + part
+            later = jnp.where((lane > step) & (lane < base + 2 * per), LOW, jnp.float32(0.0))
             to = pl.ds(pl.multiple_of(t * rows + part * half, half), half)
-            for n, mask in enumerate((0.0, first, later)):
-                query[n, to] = jnp.where(low, y, mask).astype(jnp.bfloat16)
+            query[to] = jnp.where(low, y, later).astype(jnp.bfloat16)
         return carry
 
     def prepare(t, carry):
@@ -139,9 +138,10 @@
         key_len[...] = jnp.maximum(key_len[...], lengths(kv, key_half))
         low = low_lanes(kv.shape)
         lane = lax.broadcasted_iota(jnp.int32, kv.shape, 1) - HEAD
-        step = 2 * (t % per) + lax.broadcasted_iota(jnp.int32, kv.shape, 0) // half
+        step = 2 * (t % (2 * per)) + lax.broadcasted_iota(jnp.int32, kv.shape, 0) // half
         is_step = jnp.where(lane == step, jnp.float32(1.0), jnp.float32(0.0))
-        key[block] = jnp.where(low, kv, is_step).astype(jnp.bfloat16)
+        key[0, block] = jnp.where(low, kv, 0.0).astype(jnp.bfloat16)
+        key[1, block] = jnp.where(low, kv, is_step).astype(jnp.bfloat16)
         value[block] = jnp.where(low, 1.0, kv).astype(jnp.bfloat16)
         acc[block] = state_in[block] if final else jnp.zeros((rows, LANES), jnp.float32)
         return carry
@@ -149,12 +149,12 @@
     query_len[...] = jnp.zeros_like(query_len)
     key_len[...] = jnp.zeros_like(key_len)
     if final:
-        lax.fori_loop(0, HEADS, prepare, 0, unroll=4)
+        lax.fori_loop(0, HEADS, prepare, 0, unroll=8)
         fetch.wait()
-        lax.fori_loop(0, HEADS, prepare_queries, 0, unroll=4)
+        lax.fori_loop(0, HEADS, prepare_queries, 0, unroll=8)
     else:
         both = lambda t, carry: prepare(t, prepare_queries(t, carry))
-        lax.fori_loop(0, HEADS, both, 0, unroll=4)
+        lax.fori_loop(0, HEADS, both, 0, unroll=8)
     longest = longest_in[0] if final else jnp.max(query_len[...])
     fits = longest * jnp.max(key_len[...]) <= SAFE * SAFE
     if final:
@@ -163,28 +163,34 @@
     else:
         longest_out[0] = jnp.where(fits, longest, -1.0)
 
-    def scores(q, j):
-        return lax.dot_general(
-            q, key[at(j)], (((1,), (1,)), ((), ())), preferred_element_type=jnp.float32
-        )
-
-    def weighted(p, j):
-        return jnp.dot(p, value[at(j)], preferred_element_type=jnp.float32)
+    def block_at(block, count=1):
+        return pl.ds(pl.multiple_of(block * rows, rows), count * rows)
+
+    def scores(q, k):
+        return lax.dot_general(q, k, (((1,), (1,)), ((), ())), preferred_element_type=jnp.float32)
+
+    def weighted(p, v):
+        return jnp.dot(p, v, preferred_element_type=jnp.float32)
 
     @pl.when(fits)
     def _():
         def weights(p, j, first):
-            diagonal = (j == first).astype(jnp.int32)
-            p[...] = jnp.exp2(scores(query[diagonal, at(first, 2)], j)).astype(jnp.bfloat16)
+            p[...] = jnp.exp2(scores(query[at(first, 2)], key[0, at(j)])).astype(jnp.bfloat16)
 
         def gather(p, j, first):
-            acc[at(first, 2)] += weighted(p[...], j)
-
-        def late_weights(p, j):
-            p[:TILE] = jnp.exp2(scores(query[2, at(j)], j)).astype(jnp.bfloat16)
-
-        def late_gather(p, j):
-            acc[at(j)] += weighted(p[:TILE], j)
+            acc[at(first, 2)] += weighted(p[...], value[at(j)])
+
+        def corner_weights(p, j, count):
+            i = per * j
+            s = scores(query[block_at(i)], key[1, block_at(i)])
+            p[:rows, :rows] = jnp.exp2(s).astype(jnp.bfloat16)
+            s = scores(query[block_at(i + 1, count - 1)], key[1, at(j)])
+            p[rows : count * rows] = jnp.exp2(s).astype(jnp.bfloat16)
+
+        def corner_gather(p, j, count):
+            i = per * j
+            acc[block_at(i)] += weighted(p[:rows, :rows], value[block_at(i)])
+            acc[block_at(i + 1, count - 1)] += weighted(p[rows : count * rows], value[at(j)])
 
         def chunk(a, carry):
             first = 2 * a
@@ -197,14 +203,22 @@
                 gather(p1, j + 1, first)
                 return carry
 
-            lax.fori_loop(0, a, turn, 0)
-            late_weights(p1, first + 1)
-            gather(p0, first, first)
+            lax.fori_loop(0, a - 1, turn, 0)
+
+            @pl.when(a > 0)
+            def _():
+                weights(p1, first - 1, first)
+                gather(p0, first - 2, first)
+                corner_weights(p0, first, 2 * per)
+                gather(p1, first - 1, first)
+
+            corner_weights(p1, first + 1, per)
+            corner_gather(p0, first, 2 * per)
             weights(p0, jnp.int32(0), jnp.minimum(first + 2, tiles - 2))
-            late_gather(p1, first + 1)
+            corner_gather(p1, first + 1, per)
             return carry
 
-        weights(p0, jnp.int32(0), jnp.int32(0))
+        corner_weights(p0, jnp.int32(0), 2 * per)
         lax.fori_loop(0, tiles // 2, chunk, 0)
 
     @pl.when(jnp.logical_not(fits))
@@ -224,11 +238,11 @@
                 top[...] = jnp.full_like(top, LOW)
 
             def key_block(j, carry):
-                s = scores(query[2 * (i == j).astype(jnp.int32), to], j)
+                s = scores(query[to], key[(i == j).astype(jnp.int32), at(j)])
                 old = top[...]
                 new = jnp.maximum(old, jnp.max(s, axis=-1, keepdims=True))
                 p = jnp.exp2(s - jnp.concatenate([new] * (TILE // LANES), axis=1))
-                acc[to] = acc[to] * jnp.exp2(old - new) + weighted(p.astype(jnp.bfloat16), j)
+                acc[to] = acc[to] * jnp.exp2(old - new) + weighted(p.astype(jnp.bfloat16), value[at(j)])
                 top[...] = new
                 return carry
 
@@ -252,7 +266,7 @@
             out_ref[t] = (num / den).astype(jnp.bfloat16)
             return carry
 
-        lax.fori_loop(0, HEADS, finish, 0, unroll=4)
+        lax.fori_loop(0, HEADS, finish, 0, unroll=8)
 
 
 def attend(*operands):
@@ -270,8 +284,8 @@
         f32_rows,
     ] * final + [
         pltpu.VMEM((TILE, LANES), jnp.float32),
-        pltpu.VMEM((3, total, LANES), jnp.bfloat16),
         bf16_rows,
+        pltpu.VMEM((2, total, LANES), jnp.bfloat16),
         bf16_rows,
         pltpu.VMEM((CHUNK, TILE), jnp.bfloat16),
         pltpu.VMEM((CHUNK, TILE), jnp.bfloat16),

time: 115 us -> 116 us (level)
  transfers between devices with their start and end apart: 6 -> 6, of which waited for: 4 -> 4; matrix products, arithmetic and copies ran while one was open for 2% -> 3% of each run, Pallas kernels for 29% -> 29%
where the time goes in v1:
time: 116 us; the launch traced here: 115 us
  Pallas kernels  61.9 us (53%)
  blocking collectives  17.1 us (15%)
  starting transfers between devices  15.9 us (14%)
  waiting for transfers between devices  11 us (9%)
  other arithmetic  3.57 us (3%)
  between operations  2.9 us (2%)
  local copies, waits for them, and re-layouts  2.4 us (2%)
    pallas_call x2, Pallas kernels, attend(): pl.pallas_call(functools.partial(attend_kernel, final), in_specs=[far, wh...  50.5 us
    all_to_all x1, blocking collectives, exchange(): return lax.all_to_all(x, 'tm', split_axis=0, concat_axis=0, tiled=True)  17.1 us
    all_to_all x2, starting transfers between devices, exchange(): return lax.all_to_all(x, 'tm', split_axis=0, concat_axis=0, tiled=True)  12 us
    pallas_call x2, Pallas kernels, project(): pl.pallas_call(functools.partial(project_kernel, with_query), grid=(width...  9.05 us
    ppermute x3, waiting for transfers between devices, same_core(): held.append(lax.ppermute(x, 'var', pairs))  6.34 us
    all_to_all x2, waiting for transfers between devices, exchange(): return lax.all_to_all(x, 'tm', split_axis=0, concat_axis=0, tiled=True)  3.94 us
    ppermute x3, starting transfers between devices, same_core(): held.append(lax.ppermute(x, 'var', pairs))  3.87 us
    unnamed x14, local copies, waits for them, and re-layouts  2.4 us
  transfers between devices with their start and end apart: 6, of which 4 were waited for; matrix products, arithmetic and copies ran while one was open for 3% of the time, Pallas kernels for 29%

profile of v1, /device:TPU:24, one launch (start us, length us, event | category | flops | bytes accessed | tf_op | source)
XLA Modules:
  0.0 114.7 jit_solution(208828370448515214)
XLA Ops:
  0.0 0.7 collective-permute-start.2
  0.7 0.9 collective-permute-start.1
  1.6 2.3 %collective-permute-start = (bf16[128,2,1024]{2,1,0:T(2,128)(2,1)}, bf16[128,2,1024]{2,1,0:T(2,128)(2,1)S(1)}, u32[]{:S(2)}, u32[]{:S(2)}) collective-permute-start(bf16[128,2,1024]{2,1,0:T(2,128)(2,1)} %refs_0_.1), channel_id=1, source_target_pairs={{0,32},{16,48},{32,64},{48,80},{64,96},{80,112},{96,0},{112,16},{1... | collective-permute-start | bytes 1572872 | tf_op jit(solution)/shard_map/ppermute | solution.py:371
  3.9 5.9 %project_own.1 = bf16[16,384,128]{2,1,0:T(8,128)(2,1)} custom-call(bf16[128,2,1024]{2,1,0:T(2,128)(2,1)} %refs_0_.1, f32[1,1024]{1,0:T(1,128)} %bitcast.17, bf16[1024,1024]{1,0:T(8,128)(2,1)} %refs_2_.3, bf16[1024,1024]{1,0:T(8,128)(2,1)} %refs_3_.3, bf16[1024,1024]{1,0:T(8,128)(2,1)} %refs_4_.1), custom_call_target="tpu_custom_call" | custom-call | flops 1610612736 | bytes 7340032 | tf_op jit(solution)/shard_map/project_own/pallas_call | solution.py:76
  9.7 8.1 %all-to-all-start = ((bf16[16,384,128]{2,1,0:T(8,128)(2,1)}), bf16[16,384,128]{2,1,0:T(8,128)(2,1)}, u32[]{:S(2)}, u32[]{:S(2)}) async-start(bf16[16,384,128]{2,1,0:T(8,128)(2,1)} %project_own.1), calls=%async_computation | async-start | bytes 3145728 | tf_op jit(solution)/shard_map/all_to_all | solution.py:22
  17.8 0.8 compare_select_fusion
  18.6 0.7 fusion
  20.6 5.7 %collective-permute-done.2 = bf16[128,2,1024]{2,1,0:T(2,128)(2,1)S(1)} collective-permute-done((bf16[128,2,1024]{2,1,0:T(2,128)(2,1)}, bf16[128,2,1024]{2,1,0:T(2,128)(2,1)S(1)}, u32[]{:S(2)}, u32[]{:S(2)}) %collective-permute-start.2) | collective-permute-done | bytes 524320 | tf_op jit(solution)/shard_map/ppermute | solution.py:371
  26.3 0.6 collective-permute-done
  26.9 0.2 copy-done.5
  27.1 0.6 copy-done.6
  27.7 0.9 broadcast_select_fusion.2
  30.2 0.7 collective-permute-done.3
  30.9 1.2 %broadcast_select_fusion.6 = bf16[32,8,1024]{2,1,0:T(8,128)(2,1)S(1)} fusion(bf16[32,8,1024]{2,1,0:T(8,128)(2,1)S(1)} %bitcast.22, pred[]{:T(512)S(6)} %eq.30, bf16[32,8,1024]{2,1,0:T(8,128)(2,1)} %bitcast.24, pred[]{:T(512)S(6)} %eq.31, bf16[32,8,1024]{2,1,0:T(8,128)(2,1)} %bitcast.26, pred[]{:T(512)S(6)} %eq.32, bf16[32,8,1024]{2,1,0:T(8,128)(2,1)S(1)} %bitcast.20, ...), kind=kLoop, calls=%fused_computation.6 | loop fusion | flops 1048576 | bytes 3145732 | tf_op jit(solution)/shard_map/jit(_where)/select_n | solution.py:360
  32.1 0.0 copy-start.1
  32.1 1.6 %copy-done.1 = bf16[1024,1024]{1,0:T(8,128)(2,1)S(1)} copy-done((bf16[1024,1024]{1,0:T(8,128)(2,1)S(1)}, bf16[1024,1024]{1,0:T(8,128)(2,1)}, u32[]{:S(2)}) %copy-start.1) | copy-done | bytes 2097176
  33.7 3.2 %project_other.1 = bf16[16,256,128]{2,1,0:T(8,128)(2,1)} custom-call(bf16[128,2,1024]{2,1,0:T(2,128)(2,1)S(1)} %bitcast.16, f32[1,1024]{1,0:T(1,128)S(1)} %bitcast.18, bf16[1024,1024]{1,0:T(8,128)(2,1)S(1)} %copy-done, bf16[1024,1024]{1,0:T(8,128)(2,1)S(1)} %copy-done.1), custom_call_target="tpu_custom_call" | custom-call | flops 1073741824 | bytes 5242880 | tf_op jit(solution)/shard_map/project_other/pallas_call | solution.py:76
  36.9 3.9 %all-to-all-done.refs_0_ = bf16[16,384,128]{2,1,0:T(8,128)(2,1)} async-done(((bf16[16,384,128]{2,1,0:T(8,128)(2,1)}), bf16[16,384,128]{2,1,0:T(8,128)(2,1)}, u32[]{:S(2)}, u32[]{:S(2)}) %all-to-all-start) | async-done | bytes 1572896 | tf_op jit(solution)/shard_map/all_to_all | solution.py:22
  40.8 3.9 %all-to-all-start.1 = ((bf16[16,256,128]{2,1,0:T(8,128)(2,1)}), bf16[16,256,128]{2,1,0:T(8,128)(2,1)S(1)}, u32[]{:S(2)}, u32[]{:S(2)}) async-start(bf16[16,256,128]{2,1,0:T(8,128)(2,1)} %project_other.1), calls=%async_computation.1 | async-start | bytes 2097152 | tf_op jit(solution)/shard_map/all_to_all | solution.py:22
  44.7 24.7 %attend_own.1 = (f32[4096,128]{1,0:T(8,128)S(1)}, f32[1]{0:T(128)}) custom-call(bf16[16,384,128]{2,1,0:T(8,128)(2,1)} %all-to-all-done.refs_0_), custom_call_target="tpu_custom_call" | custom-call | flops 17179869184 | bytes 8388608 | tf_op jit(solution)/shard_map/attend_own/pallas_call | solution.py:303
  69.5 0.0 copy-start.2
  69.5 25.8 %attend_other.1 = bf16[16,128,128]{2,1,0:T(8,128)(2,1)S(1)} custom-call(bf16[16,384,128]{2,1,0:T(8,128)(2,1)} %all-to-all-done.refs_0_, bf16[16,256,128]{2,1,0:T(8,128)(2,1)S(1)} %all-to-all-done.1.refs_1_, f32[4096,128]{1,0:T(8,128)S(1)} %get-tuple-element.15.refs_2_, f32[1]{0:T(128)} %get-tuple-element.16.refs_3_), custom_call_target="tpu_custom_call" | custom-call | flops 17179869184 | bytes 8388608 | tf_op jit(solution)/shard_map/attend_other/pallas_call | solution.py:303
  95.3 17.1 %all_to_all.15.a_ref = bf16[16,128,128]{2,1,0:T(8,128)(2,1)S(1)} all-to-all(bf16[16,128,128]{2,1,0:T(8,128)(2,1)S(1)} %attend_other.1), channel_id=1, replica_groups=mesh['var'=8,'tm'=16] {'tm'}, dimensions={0} | all-to-all | bytes 1048576 | tf_op jit(solution)/shard_map/all_to_all | solution.py:22
  112.4 2.3 %project_out.1 = bf16[128,2,1024]{2,1,0:T(2,128)(2,1)} custom-call(bf16[16,128,128]{2,1,0:T(8,128)(2,1)S(1)} %all_to_all.15.a_ref, bf16[1024,1024]{1,0:T(8,128)(2,1)S(1)} %copy-done.2), custom_call_target="tpu_custom_call" | custom-call | flops 536870912 | bytes 2097152 | tf_op jit(solution)/shard_map/project_out/pallas_call | solution.py:337
  (12 shorter events, 0.0 us)
Async XLA Ops:
  0.0 26.3 %collective-permute-start.2 = (bf16[128,2,1024]{2,1,0:T(2,128)(2,1)}, bf16[128,2,1024]{2,1,0:T(2,128)(2,1)S(1)}, u32[]{:S(2)}, u32[]{:S(2)}) collective-permute-start(bf16[128,2,1024]{2,1,0:T(2,128)(2,1)} %refs_0_.1), channel_id=1, source_target_pairs={{0,96},{16,112},{32,0},{48,16},{64,32},{80,48},{96,64},{112,80},{1... | collective-permute-start | bytes 1572872 | tf_op jit(solution)/shard_map/ppermute | solution.py:371
  0.7 25.6 %collective-permute-start.1 = (bf16[128,2,1024]{2,1,0:T(2,128)(2,1)}, bf16[128,2,1024]{2,1,0:T(2,128)(2,1)S(1)}, u32[]{:S(2)}, u32[]{:S(2)}) collective-permute-start(bf16[128,2,1024]{2,1,0:T(2,128)(2,1)} %refs_0_.1), channel_id=1, source_target_pairs={{0,64},{16,80},{32,96},{48,112},{64,0},{80,16},{96,32},{112,48},{1... | collective-permute-start | bytes 1572872 | tf_op jit(solution)/shard_map/ppermute | solution.py:371
  1.6 25.3 %collective-permute-start = (bf16[128,2,1024]{2,1,0:T(2,128)(2,1)}, bf16[128,2,1024]{2,1,0:T(2,128)(2,1)S(1)}, u32[]{:S(2)}, u32[]{:S(2)}) collective-permute-start(bf16[128,2,1024]{2,1,0:T(2,128)(2,1)} %refs_0_.1), channel_id=1, source_target_pairs={{0,32},{16,48},{32,64},{48,80},{64,96},{80,112},{96,0},{112,16},{1... | collective-permute-start | bytes 1572872 | tf_op jit(solution)/shard_map/ppermute | solution.py:371
  9.7 18.0 %copy-start.4 = (bf16[128,2,1024]{2,1,0:T(2,128)(2,1)S(1)}, bf16[128,2,1024]{2,1,0:T(2,128)(2,1)}, u32[]{:S(2)}) copy-start(bf16[128,2,1024]{2,1,0:T(2,128)(2,1)} %refs_0_.1) | copy-start | bytes 1572868
  9.7 31.1 %all-to-all-start = ((bf16[16,384,128]{2,1,0:T(8,128)(2,1)}), bf16[16,384,128]{2,1,0:T(8,128)(2,1)}, u32[]{:S(2)}, u32[]{:S(2)}) async-start(bf16[16,384,128]{2,1,0:T(8,128)(2,1)} %project_own.1), calls=%async_computation | async-start | bytes 3145728 | tf_op jit(solution)/shard_map/all_to_all | solution.py:22
  26.3 0.8 copy-start.5
  26.9 0.8 copy-start.6
  28.6 3.4 %copy-start = (bf16[1024,1024]{1,0:T(8,128)(2,1)S(1)}, bf16[1024,1024]{1,0:T(8,128)(2,1)}, u32[]{:S(2)}) copy-start(bf16[1024,1024]{1,0:T(8,128)(2,1)} %refs_2_.3) | copy-start | bytes 6291460
  28.6 3.4 %copy-start.3 = (f32[1024]{0:T(1024)S(1)}, f32[1024]{0:T(1024)}, u32[]{:S(2)}) copy-start(f32[1024]{0:T(1024)} %param.8) | copy-start | bytes 12292
  28.6 2.3 %collective-permute-start.3 = (bf16[128,2,1024]{2,1,0:T(2,128)(2,1)}, bf16[128,2,1024]{2,1,0:T(2,128)(2,1)}, u32[]{:S(2)}, u32[]{:S(2)}) collective-permute-start(bf16[128,2,1024]{2,1,0:T(2,128)(2,1)} %bitcast.9), channel_id=1, source_target_pairs={{0,16},{16,0},{32,48},{48,32},{64,80},{80,64},{96,112},{112,96},{1... | collective-permute-start | bytes 1572872 | tf_op jit(solution)/shard_map/ppermute | solution.py:383
  32.1 1.6 %copy-start.1 = (bf16[1024,1024]{1,0:T(8,128)(2,1)S(1)}, bf16[1024,1024]{1,0:T(8,128)(2,1)}, u32[]{:S(2)}) copy-start(bf16[1024,1024]{1,0:T(8,128)(2,1)} %refs_3_.3) | copy-start | bytes 6291460
  40.8 28.7 %all-to-all-start.1 = ((bf16[16,256,128]{2,1,0:T(8,128)(2,1)}), bf16[16,256,128]{2,1,0:T(8,128)(2,1)S(1)}, u32[]{:S(2)}, u32[]{:S(2)}) async-start(bf16[16,256,128]{2,1,0:T(8,128)(2,1)} %project_other.1), calls=%async_computation.1 | async-start | bytes 2097152 | tf_op jit(solution)/shard_map/all_to_all | solution.py:22
  69.5 42.9 %copy-start.2 = (bf16[1024,1024]{1,0:T(8,128)(2,1)S(1)}, bf16[1024,1024]{1,0:T(8,128)(2,1)}, u32[]{:S(2)}) copy-start(bf16[1024,1024]{1,0:T(8,128)(2,1)} %w_ref.1) | copy-start | bytes 6291460

commit v2 on v1

--- a/solution.py
+++ b/solution.py
@@ -94,17 +94,14 @@
 
 
 def attend_kernel(final, *refs):
-    q_ref, *refs = refs
-    kv_ref = q_ref
-    if final:
-        q_far = q_ref
-        kv_ref, state_in, longest_in, out_ref, q_ref, sem, acc, *refs = refs
-        fetch = pltpu.make_async_copy(q_far.at[:, kv_ref.shape[1] :], q_ref, sem.at[0])
-        fetch.start()
+    if final:
+        kv_ref, query, state_in, longest_in, out_ref, acc, *refs = refs
+        rows = kv_ref.shape[1]
     else:
-        acc, longest_out, *refs = refs
-    top, query, key, value, p0, p1, query_len, key_len = refs
-    rows = kv_ref.shape[1] if final else q_ref.shape[1] * 2 // 3
+        q_ref, acc, query, longest_out, *refs = refs
+        kv_ref = q_ref
+        rows = q_ref.shape[1] * 2 // 3
+    top, key, value, p0, p1, query_len, key_len = refs
     half = rows // 2
     per = TILE // rows
     tiles = HEADS // per
@@ -119,9 +116,8 @@
         return pl.ds(pl.multiple_of(tile * TILE, TILE), count * TILE)
 
     def prepare_queries(t, carry):
-        x = q_ref[t, (0 if final else rows) :].astype(jnp.float32)
-        if not final:
-            query_len[...] = jnp.maximum(query_len[...], lengths(x, same_half))
+        x = q_ref[t, rows:].astype(jnp.float32)
+        query_len[...] = jnp.maximum(query_len[...], lengths(x, same_half))
         low = low_lanes(x.shape)
         lane = lax.broadcasted_iota(jnp.int32, x.shape, 1) - HEAD
         base = 2 * per * (t // per % 2)
@@ -150,8 +146,6 @@
     key_len[...] = jnp.zeros_like(key_len)
     if final:
         lax.fori_loop(0, HEADS, prepare, 0, unroll=8)
-        fetch.wait()
-        lax.fori_loop(0, HEADS, prepare_queries, 0, unroll=8)
     else:
         both = lambda t, carry: prepare(t, prepare_queries(t, carry))
         lax.fori_loop(0, HEADS, both, 0, unroll=8)
@@ -270,21 +264,15 @@
 
 
 def attend(*operands):
-    rows = operands[0].shape[1] * 2 // 3
     final = len(operands) > 1
+    rows = operands[0].shape[1] if final else operands[0].shape[1] * 2 // 3
     total = HEADS * rows
     whole = pl.BlockSpec(memory_space=pltpu.VMEM)
     scalar = pl.BlockSpec(memory_space=pltpu.SMEM)
-    far = pl.BlockSpec(memory_space=pl.ANY)
     bf16_rows = pltpu.VMEM((total, LANES), jnp.bfloat16)
     f32_rows = pltpu.VMEM((total, LANES), jnp.float32)
-    scratch = [
-        pltpu.VMEM((HEADS, rows // 2, LANES), jnp.bfloat16),
-        pltpu.SemaphoreType.DMA((1,)),
-        f32_rows,
-    ] * final + [
+    scratch = [f32_rows] * final + [
         pltpu.VMEM((TILE, LANES), jnp.float32),
-        bf16_rows,
         pltpu.VMEM((2, total, LANES), jnp.bfloat16),
         bf16_rows,
         pltpu.VMEM((CHUNK, TILE), jnp.bfloat16),
@@ -297,13 +285,14 @@
     else:
         out = [
             jax.ShapeDtypeStruct((total, LANES), jnp.float32),
+            jax.ShapeDtypeStruct((total, LANES), jnp.bfloat16),
             jax.ShapeDtypeStruct((1,), jnp.float32),
         ]
     pairs = total * total // 2
     return pl.pallas_call(
         functools.partial(attend_kernel, final),
-        in_specs=[far, whole, whole, scalar] if final else [whole],
-        out_specs=whole if final else [whole, scalar],
+        in_specs=[whole, whole, whole, scalar] if final else [whole],
+        out_specs=whole if final else [whole, whole, scalar],
         out_shape=out,
         scratch_shapes=scratch,
         compiler_params=pltpu.CompilerParams(vmem_limit_bytes=20 << 20),
@@ -394,7 +383,8 @@
     kv_other = project(x_other, gain, (w_key, w_value))
     packed, _ = lax.optimization_barrier((exchange(packed), kv_other))
     kv_other = exchange(kv_other)
-    att = exchange(attend(packed, kv_other, *attend(packed)))
+    state, query, longest = attend(packed)
+    att = exchange(attend(kv_other, query, state, longest))
     return project_out(att, w_out)
 
 

time: 116 us -> 118 us (1.017)
  local copies, waits for them, and re-layouts: 2.4 us -> 4.59 us
    unnamed x14 -> x18, local copies, waits for them, and re-layouts: 2.4 us -> 4.59 us
where the time goes in v2:
time: 118 us; the launch traced here: 117 us
  Pallas kernels  61.4 us (52%)
  blocking collectives  17.1 us (14%)
  starting transfers between devices  15.9 us (13%)
  waiting for transfers between devices  11 us (9%)
  local copies, waits for them, and re-layouts  4.59 us (4%)
  other arithmetic  3.59 us (3%)
  between operations  2.9 us (2%)
    pallas_call x2, Pallas kernels, attend(): pl.pallas_call(functools.partial(attend_kernel, final), in_specs=[whole,...  50.1 us
    all_to_all x1, blocking collectives, exchange(): return lax.all_to_all(x, 'tm', split_axis=0, concat_axis=0, tiled=True)  17.1 us
    all_to_all x2, starting transfers between devices, exchange(): return lax.all_to_all(x, 'tm', split_axis=0, concat_axis=0, tiled=True)  12 us
    pallas_call x2, Pallas kernels, project(): pl.pallas_call(functools.partial(project_kernel, with_query), grid=(width...  9.04 us
    ppermute x3, waiting for transfers between devices, same_core(): held.append(lax.ppermute(x, 'var', pairs))  6.27 us
    unnamed x18, local copies, waits for them, and re-layouts  4.59 us
    all_to_all x2, waiting for transfers between devices, exchange(): return lax.all_to_all(x, 'tm', split_axis=0, concat_axis=0, tiled=True)  3.92 us
    ppermute x3, starting transfers between devices, same_core(): held.append(lax.ppermute(x, 'var', pairs))  3.87 us
  transfers between devices with their start and end apart: 6, of which 4 were waited for; matrix products, arithmetic and copies ran while one was open for 3% of the time, Pallas kernels for 29%

profile of v2, /device:TPU:24, one launch (start us, length us, event | category | flops | bytes accessed | tf_op | source)
XLA Modules:
  0.0 116.5 jit_solution(1739407731168104201)
XLA Ops:
  0.0 0.7 collective-permute-start.2
  0.7 0.9 collective-permute-start.1
  1.6 2.3 %collective-permute-start = (bf16[128,2,1024]{2,1,0:T(2,128)(2,1)}, bf16[128,2,1024]{2,1,0:T(2,128)(2,1)S(1)}, u32[]{:S(2)}, u32[]{:S(2)}) collective-permute-start(bf16[128,2,1024]{2,1,0:T(2,128)(2,1)} %refs_0_.1), channel_id=1, source_target_pairs={{0,32},{16,48},{32,64},{48,80},{64,96},{80,112},{96,0},{112,16},{1... | collective-permute-start | bytes 1572872 | tf_op jit(solution)/shard_map/ppermute | solution.py:360
  3.9 5.9 %project_own.1 = bf16[16,384,128]{2,1,0:T(8,128)(2,1)} custom-call(bf16[128,2,1024]{2,1,0:T(2,128)(2,1)} %refs_0_.1, f32[1,1024]{1,0:T(1,128)} %bitcast.17, bf16[1024,1024]{1,0:T(8,128)(2,1)} %refs_2_.3, bf16[1024,1024]{1,0:T(8,128)(2,1)} %refs_3_.3, bf16[1024,1024]{1,0:T(8,128)(2,1)} %refs_4_.1), custom_call_target="tpu_custom_call" | custom-call | flops 1610612736 | bytes 7340032 | tf_op jit(solution)/shard_map/project_own/pallas_call | solution.py:76
  9.7 8.1 %all-to-all-start.1 = ((bf16[16,384,128]{2,1,0:T(8,128)(2,1)}), bf16[16,384,128]{2,1,0:T(8,128)(2,1)}, u32[]{:S(2)}, u32[]{:S(2)}) async-start(bf16[16,384,128]{2,1,0:T(8,128)(2,1)} %project_own.1), calls=%async_computation.1 | async-start | bytes 3145728 | tf_op jit(solution)/shard_map/all_to_all | solution.py:22
  17.8 0.8 compare_select_fusion
  18.6 0.7 fusion
  20.7 5.7 %collective-permute-done.2 = bf16[128,2,1024]{2,1,0:T(2,128)(2,1)S(1)} collective-permute-done((bf16[128,2,1024]{2,1,0:T(2,128)(2,1)}, bf16[128,2,1024]{2,1,0:T(2,128)(2,1)S(1)}, u32[]{:S(2)}, u32[]{:S(2)}) %collective-permute-start.2) | collective-permute-done | bytes 524320 | tf_op jit(solution)/shard_map/ppermute | solution.py:360
  26.3 0.6 collective-permute-done
  26.9 0.2 copy-done.7
  27.1 0.6 copy-done.8
  27.7 0.9 broadcast_select_fusion.2
  30.1 0.8 collective-permute-done.3
  30.9 1.2 broadcast_select_fusion.6
  32.1 1.6 %copy-done.1 = bf16[1024,1024]{1,0:T(8,128)(2,1)S(1)} copy-done((bf16[1024,1024]{1,0:T(8,128)(2,1)S(1)}, bf16[1024,1024]{1,0:T(8,128)(2,1)}, u32[]{:S(2)}) %copy-start.1) | copy-done | bytes 2097176
  33.7 3.2 %project_other.1 = bf16[16,256,128]{2,1,0:T(8,128)(2,1)} custom-call(bf16[128,2,1024]{2,1,0:T(2,128)(2,1)S(1)} %bitcast.16, f32[1,1024]{1,0:T(1,128)S(1)} %bitcast.18, bf16[1024,1024]{1,0:T(8,128)(2,1)S(1)} %copy-done, bf16[1024,1024]{1,0:T(8,128)(2,1)S(1)} %copy-done.1), custom_call_target="tpu_custom_call" | custom-call | flops 1073741824 | bytes 5242880 | tf_op jit(solution)/shard_map/project_other/pallas_call | solution.py:76
  36.9 3.9 %all-to-all-done.1.refs_0_ = bf16[16,384,128]{2,1,0:T(8,128)(2,1)} async-done(((bf16[16,384,128]{2,1,0:T(8,128)(2,1)}), bf16[16,384,128]{2,1,0:T(8,128)(2,1)}, u32[]{:S(2)}, u32[]{:S(2)}) %all-to-all-start.1) | async-done | bytes 1572896 | tf_op jit(solution)/shard_map/all_to_all | solution.py:22
  40.8 4.0 %all-to-all-start = ((bf16[16,256,128]{2,1,0:T(8,128)(2,1)}), bf16[16,256,128]{2,1,0:T(8,128)(2,1)S(1)}, u32[]{:S(2)}, u32[]{:S(2)}) async-start(bf16[16,256,128]{2,1,0:T(8,128)(2,1)} %project_other.1), calls=%async_computation | async-start | bytes 2097152 | tf_op jit(solution)/shard_map/all_to_all | solution.py:22
  44.8 24.7 %attend_own.1 = (f32[4096,128]{1,0:T(8,128)S(1)}, bf16[4096,128]{1,0:T(8,128)(2,1)S(1)}, f32[1]{0:T(128)}) custom-call(bf16[16,384,128]{2,1,0:T(8,128)(2,1)} %all-to-all-done.1.refs_0_), custom_call_target="tpu_custom_call" | custom-call | flops 17179869184 | bytes 8388608 | tf_op jit(solution)/shard_map/attend_own/pallas_call | solution.py:292
  69.5 1.0 copy-done.4
  70.4 1.2 %copy-done.5 = bf16[4096,128]{1,0:T(8,128)(2,1)S(1)} copy-done((bf16[4096,128]{1,0:T(8,128)(2,1)S(1)}, bf16[4096,128]{1,0:T(8,128)(2,1)}, u32[]{:S(2)}) %copy-start.5) | copy-done | bytes 1048600
  71.7 25.4 %attend_other.1 = bf16[16,128,128]{2,1,0:T(8,128)(2,1)S(1)} custom-call(bf16[16,256,128]{2,1,0:T(8,128)(2,1)S(1)} %all-to-all-done.refs_0_, bf16[4096,128]{1,0:T(8,128)(2,1)S(1)} %copy-done.5, f32[4096,128]{1,0:T(8,128)S(1)} %get-tuple-element.17.refs_2_, f32[1]{0:T(128)} %get-tuple-element.18.refs_3_), custom_call_target="tpu_custom_call" | custom-call | flops 17179869184 | bytes 8388608 | tf_op jit(solution)/shard_map/attend_other/pallas_call | solution.py:292
  97.1 17.1 %all_to_all.15.a_ref = bf16[16,128,128]{2,1,0:T(8,128)(2,1)S(1)} all-to-all(bf16[16,128,128]{2,1,0:T(8,128)(2,1)S(1)} %attend_other.1), channel_id=1, replica_groups=mesh['var'=8,'tm'=16] {'tm'}, dimensions={0} | all-to-all | bytes 1048576 | tf_op jit(solution)/shard_map/all_to_all | solution.py:22
  114.2 2.3 %project_out.1 = bf16[128,2,1024]{2,1,0:T(2,128)(2,1)} custom-call(bf16[16,128,128]{2,1,0:T(8,128)(2,1)S(1)} %all_to_all.15.a_ref, bf16[1024,1024]{1,0:T(8,128)(2,1)S(1)} %copy-done.2), custom_call_target="tpu_custom_call" | custom-call | flops 536870912 | bytes 2097152 | tf_op jit(solution)/shard_map/project_out/pallas_call | solution.py:326
  (16 shorter events, 0.0 us)
Async XLA Ops:
  0.0 26.3 %collective-permute-start.2 = (bf16[128,2,1024]{2,1,0:T(2,128)(2,1)}, bf16[128,2,1024]{2,1,0:T(2,128)(2,1)S(1)}, u32[]{:S(2)}, u32[]{:S(2)}) collective-permute-start(bf16[128,2,1024]{2,1,0:T(2,128)(2,1)} %refs_0_.1), channel_id=1, source_target_pairs={{0,96},{16,112},{32,0},{48,16},{64,32},{80,48},{96,64},{112,80},{1... | collective-permute-start | bytes 1572872 | tf_op jit(solution)/shard_map/ppermute | solution.py:360
  0.7 25.6 %collective-permute-start.1 = (bf16[128,2,1024]{2,1,0:T(2,128)(2,1)}, bf16[128,2,1024]{2,1,0:T(2,128)(2,1)S(1)}, u32[]{:S(2)}, u32[]{:S(2)}) collective-permute-start(bf16[128,2,1024]{2,1,0:T(2,128)(2,1)} %refs_0_.1), channel_id=1, source_target_pairs={{0,64},{16,80},{32,96},{48,112},{64,0},{80,16},{96,32},{112,48},{1... | collective-permute-start | bytes 1572872 | tf_op jit(solution)/shard_map/ppermute | solution.py:360
  1.6 25.3 %collective-permute-start = (bf16[128,2,1024]{2,1,0:T(2,128)(2,1)}, bf16[128,2,1024]{2,1,0:T(2,128)(2,1)S(1)}, u32[]{:S(2)}, u32[]{:S(2)}) collective-permute-start(bf16[128,2,1024]{2,1,0:T(2,128)(2,1)} %refs_0_.1), channel_id=1, source_target_pairs={{0,32},{16,48},{32,64},{48,80},{64,96},{80,112},{96,0},{112,16},{1... | collective-permute-start | bytes 1572872 | tf_op jit(solution)/shard_map/ppermute | solution.py:360
  9.7 18.0 %copy-start.6 = (bf16[128,2,1024]{2,1,0:T(2,128)(2,1)S(1)}, bf16[128,2,1024]{2,1,0:T(2,128)(2,1)}, u32[]{:S(2)}) copy-start(bf16[128,2,1024]{2,1,0:T(2,128)(2,1)} %refs_0_.1) | copy-start | bytes 1572868
  9.7 31.1 %all-to-all-start.1 = ((bf16[16,384,128]{2,1,0:T(8,128)(2,1)}), bf16[16,384,128]{2,1,0:T(8,128)(2,1)}, u32[]{:S(2)}, u32[]{:S(2)}) async-start(bf16[16,384,128]{2,1,0:T(8,128)(2,1)} %project_own.1), calls=%async_computation.1 | async-start | bytes 3145728 | tf_op jit(solution)/shard_map/all_to_all | solution.py:22
  26.3 0.8 copy-start.7
  26.9 0.8 copy-start.8
  28.7 3.4 %copy-start = (bf16[1024,1024]{1,0:T(8,128)(2,1)S(1)}, bf16[1024,1024]{1,0:T(8,128)(2,1)}, u32[]{:S(2)}) copy-start(bf16[1024,1024]{1,0:T(8,128)(2,1)} %refs_2_.3) | copy-start | bytes 6291460
  28.7 3.4 %copy-start.3 = (f32[1024]{0:T(1024)S(1)}, f32[1024]{0:T(1024)}, u32[]{:S(2)}) copy-start(f32[1024]{0:T(1024)} %param.8) | copy-start | bytes 12292
  28.7 2.3 %collective-permute-start.3 = (bf16[128,2,1024]{2,1,0:T(2,128)(2,1)}, bf16[128,2,1024]{2,1,0:T(2,128)(2,1)}, u32[]{:S(2)}, u32[]{:S(2)}) collective-permute-start(bf16[128,2,1024]{2,1,0:T(2,128)(2,1)} %bitcast.9), channel_id=1, source_target_pairs={{0,16},{16,0},{32,48},{48,32},{64,80},{80,64},{96,112},{112,96},{1... | collective-permute-start | bytes 1572872 | tf_op jit(solution)/shard_map/ppermute | solution.py:372
  32.1 1.6 %copy-start.1 = (bf16[1024,1024]{1,0:T(8,128)(2,1)S(1)}, bf16[1024,1024]{1,0:T(8,128)(2,1)}, u32[]{:S(2)}) copy-start(bf16[1024,1024]{1,0:T(8,128)(2,1)} %refs_3_.3) | copy-start | bytes 6291460
  40.8 29.6 %all-to-all-start = ((bf16[16,256,128]{2,1,0:T(8,128)(2,1)}), bf16[16,256,128]{2,1,0:T(8,128)(2,1)S(1)}, u32[]{:S(2)}, u32[]{:S(2)}) async-start(bf16[16,256,128]{2,1,0:T(8,128)(2,1)} %project_other.1), calls=%async_computation | async-start | bytes 2097152 | tf_op jit(solution)/shard_map/all_to_all | solution.py:22
  69.5 1.0 copy-start.4
  70.4 1.2 %copy-start.5 = (bf16[4096,128]{1,0:T(8,128)(2,1)S(1)}, bf16[4096,128]{1,0:T(8,128)(2,1)}, u32[]{:S(2)}) copy-start(bf16[4096,128]{1,0:T(8,128)(2,1)} %copy-done.4) | copy-start | bytes 3145732
  71.7 42.5 %copy-start.2 = (bf16[1024,1024]{1,0:T(8,128)(2,1)S(1)}, bf16[1024,1024]{1,0:T(8,128)(2,1)}, u32[]{:S(2)}) copy-start(bf16[1024,1024]{1,0:T(8,128)(2,1)} %w_ref.1) | copy-start | bytes 6291460

commit v3 on v1

--- a/solution.py
+++ b/solution.py
@@ -174,52 +174,36 @@
 
     @pl.when(fits)
     def _():
-        def weights(p, j, first):
-            p[...] = jnp.exp2(scores(query[at(first, 2)], key[0, at(j)])).astype(jnp.bfloat16)
-
-        def gather(p, j, first):
-            acc[at(first, 2)] += weighted(p[...], value[at(j)])
-
-        def corner_weights(p, j, count):
-            i = per * j
-            s = scores(query[block_at(i)], key[1, block_at(i)])
-            p[:rows, :rows] = jnp.exp2(s).astype(jnp.bfloat16)
-            s = scores(query[block_at(i + 1, count - 1)], key[1, at(j)])
-            p[rows : count * rows] = jnp.exp2(s).astype(jnp.bfloat16)
-
-        def corner_gather(p, j, count):
-            i = per * j
-            acc[block_at(i)] += weighted(p[:rows, :rows], value[block_at(i)])
-            acc[block_at(i + 1, count - 1)] += weighted(p[rows : count * rows], value[at(j)])
-
-        def chunk(a, carry):
-            first = 2 * a
-
-            def turn(n, carry):
-                j = 2 * n
-                weights(p1, j + 1, first)
-                gather(p0, j, first)
-                weights(p0, j + 2, first)
-                gather(p1, j + 1, first)
-                return carry
-
-            lax.fori_loop(0, a - 1, turn, 0)
-
-            @pl.when(a > 0)
-            def _():
-                weights(p1, first - 1, first)
-                gather(p0, first - 2, first)
-                corner_weights(p0, first, 2 * per)
-                gather(p1, first - 1, first)
-
-            corner_weights(p1, first + 1, per)
-            corner_gather(p0, first, 2 * per)
-            weights(p0, jnp.int32(0), jnp.minimum(first + 2, tiles - 2))
-            corner_gather(p1, first + 1, per)
-            return carry
-
-        corner_weights(p0, jnp.int32(0), 2 * per)
-        lax.fori_loop(0, tiles // 2, chunk, 0)
+        def spans(first, j):
+            start, diagonal = first * per, j >= first
+            if not diagonal:
+                return [(0, start, 2 * per, j * per, per)]
+            corner = j * per
+            return [
+                (0, corner, 1, corner, 1),
+                (1, corner + 1, start + 2 * per - corner - 1, corner, per),
+            ]
+
+        def weights(p, first, j):
+            version = int(j >= first)
+            for at_row, row, count, column, width in spans(first, j):
+                s = scores(query[block_at(row, count)], key[version, block_at(column, width)])
+                here = slice(at_row * rows, (at_row + count) * rows)
+                p[here, : width * rows] = jnp.exp2(s).astype(jnp.bfloat16)
+
+        def gather(p, first, j):
+            for at_row, row, count, column, width in spans(first, j):
+                here = slice(at_row * rows, (at_row + count) * rows)
+                v = value[block_at(column, width)]
+                acc[block_at(row, count)] += weighted(p[here, : width * rows], v)
+
+        todo = [(first, j) for first in range(0, tiles, 2) for j in range(first + 2)]
+        slots = (p0, p1)
+        weights(p0, *todo[0])
+        for n, here in enumerate(todo):
+            if n + 1 < len(todo):
+                weights(slots[(n + 1) % 2], *todo[n + 1])
+            gather(slots[n % 2], *here)
 
     @pl.when(jnp.logical_not(fits))
     def _():

time: 116 us -> 118 us (1.017)
  the two profiles are of different devices: /device:TPU:24 before, /device:TPU:1 now
where the time goes in v3:
time: 118 us; the launch traced here: 115 us
  Pallas kernels  62.1 us (53%)
  starting transfers between devices  20.4 us (17%)
  blocking collectives  15.4 us (13%)
  waiting for transfers between devices  9.72 us (8%)
  between operations  2.94 us (2%)
  other arithmetic  2.53 us (2%)
  local copies, waits for them, and re-layouts  2.4 us (2%)
    pallas_call x2, Pallas kernels, attend(): pl.pallas_call(functools.partial(attend_kernel, final), in_specs=[far, wh...  50.7 us
    all_to_all x1, blocking collectives, exchange(): return lax.all_to_all(x, 'tm', split_axis=0, concat_axis=0, tiled=True)  15.4 us
    all_to_all x2, starting transfers between devices, exchange(): return lax.all_to_all(x, 'tm', split_axis=0, concat_axis=0, tiled=True)  15.4 us
    ppermute x3, waiting for transfers between devices, same_core(): held.append(lax.ppermute(x, 'var', pairs))  9.41 us
    pallas_call x2, Pallas kernels, project(): pl.pallas_call(functools.partial(project_kernel, with_query), grid=(width...  9.05 us
    ppermute x3, starting transfers between devices, same_core(): held.append(lax.ppermute(x, 'var', pairs))  4.6 us
    unnamed x14, local copies, waits for them, and re-layouts  2.4 us
  transfers between devices with their start and end apart: 6, of which 3 were waited for; matrix products, arithmetic and copies ran while one was open for 2% of the time, Pallas kernels for 29%

profile of v3, /device:TPU:1, one launch (start us, length us, event | category | flops | bytes accessed | tf_op | source)
XLA Modules:
  0.0 115.5 jit_solution(10551866726342927730)
XLA Ops:
  0.0 3.6 %collective-permute-start.2 = (bf16[128,2,1024]{2,1,0:T(2,128)(2,1)}, bf16[128,2,1024]{2,1,0:T(2,128)(2,1)S(1)}, u32[]{:S(2)}, u32[]{:S(2)}) collective-permute-start(bf16[128,2,1024]{2,1,0:T(2,128)(2,1)} %refs_0_.1), channel_id=1, source_target_pairs={{0,96},{16,112},{32,0},{48,16},{64,32},{80,48},{96,64},{112,80},{1... | collective-permute-start | bytes 1572872 | tf_op jit(solution)/shard_map/ppermute | solution.py:355
  3.6 0.3 collective-permute-start.1
  3.9 0.7 collective-permute-start
  4.6 5.9 %project_own.1 = bf16[16,384,128]{2,1,0:T(8,128)(2,1)} custom-call(bf16[128,2,1024]{2,1,0:T(2,128)(2,1)} %refs_0_.1, f32[1,1024]{1,0:T(1,128)} %bitcast.17, bf16[1024,1024]{1,0:T(8,128)(2,1)} %refs_2_.3, bf16[1024,1024]{1,0:T(8,128)(2,1)} %refs_3_.3, bf16[1024,1024]{1,0:T(8,128)(2,1)} %refs_4_.1), custom_call_target="tpu_custom_call" | custom-call | flops 1610612736 | bytes 7340032 | tf_op jit(solution)/shard_map/project_own/pallas_call | solution.py:76
  10.5 7.8 %all-to-all-start = ((bf16[16,384,128]{2,1,0:T(8,128)(2,1)}), bf16[16,384,128]{2,1,0:T(8,128)(2,1)}, u32[]{:S(2)}, u32[]{:S(2)}) async-start(bf16[16,384,128]{2,1,0:T(8,128)(2,1)} %project_own.1), calls=%async_computation | async-start | bytes 3145728 | tf_op jit(solution)/shard_map/all_to_all | solution.py:22
  18.3 0.8 compare_select_fusion
  19.0 0.7 fusion
  21.1 4.5 %collective-permute-done.2 = bf16[128,2,1024]{2,1,0:T(2,128)(2,1)S(1)} collective-permute-done((bf16[128,2,1024]{2,1,0:T(2,128)(2,1)}, bf16[128,2,1024]{2,1,0:T(2,128)(2,1)S(1)}, u32[]{:S(2)}, u32[]{:S(2)}) %collective-permute-start.2) | collective-permute-done | bytes 524320 | tf_op jit(solution)/shard_map/ppermute | solution.py:355
  25.6 0.0 collective-permute-done.1
  25.6 4.9 %collective-permute-done = bf16[128,2,1024]{2,1,0:T(2,128)(2,1)S(1)} collective-permute-done((bf16[128,2,1024]{2,1,0:T(2,128)(2,1)}, bf16[128,2,1024]{2,1,0:T(2,128)(2,1)S(1)}, u32[]{:S(2)}, u32[]{:S(2)}) %collective-permute-start) | collective-permute-done | bytes 524320 | tf_op jit(solution)/shard_map/ppermute | solution.py:355
  30.5 0.8 copy-done.6
  31.3 0.9 broadcast_select_fusion.2
  32.2 0.4 collective-permute-start.3
  34.1 0.3 collective-permute-done.3
  34.4 0.1 broadcast_select_fusion.6
  34.6 0.0 copy-start.1
  34.6 1.6 %copy-done.1 = bf16[1024,1024]{1,0:T(8,128)(2,1)S(1)} copy-done((bf16[1024,1024]{1,0:T(8,128)(2,1)S(1)}, bf16[1024,1024]{1,0:T(8,128)(2,1)}, u32[]{:S(2)}) %copy-start.1) | copy-done | bytes 2097176
  36.2 3.2 %project_other.1 = bf16[16,256,128]{2,1,0:T(8,128)(2,1)} custom-call(bf16[128,2,1024]{2,1,0:T(2,128)(2,1)S(1)} %bitcast.16, f32[1,1024]{1,0:T(1,128)S(1)} %bitcast.18, bf16[1024,1024]{1,0:T(8,128)(2,1)S(1)} %copy-done, bf16[1024,1024]{1,0:T(8,128)(2,1)S(1)} %copy-done.1), custom_call_target="tpu_custom_call" | custom-call | flops 1073741824 | bytes 5242880 | tf_op jit(solution)/shard_map/project_other/pallas_call | solution.py:76
  39.4 7.6 %all-to-all-start.1 = ((bf16[16,256,128]{2,1,0:T(8,128)(2,1)}), bf16[16,256,128]{2,1,0:T(8,128)(2,1)S(1)}, u32[]{:S(2)}, u32[]{:S(2)}) async-start(bf16[16,256,128]{2,1,0:T(8,128)(2,1)} %project_other.1), calls=%async_computation.1 | async-start | bytes 2097152 | tf_op jit(solution)/shard_map/all_to_all | solution.py:22
  47.0 24.9 %attend_own.1 = (f32[4096,128]{1,0:T(8,128)S(1)}, f32[1]{0:T(128)}) custom-call(bf16[16,384,128]{2,1,0:T(8,128)(2,1)} %all-to-all-done.refs_0_), custom_call_target="tpu_custom_call" | custom-call | flops 17179869184 | bytes 8388608 | tf_op jit(solution)/shard_map/attend_own/pallas_call | solution.py:287
  71.9 0.0 copy-start.2
  71.9 25.8 %attend_other.1 = bf16[16,128,128]{2,1,0:T(8,128)(2,1)S(1)} custom-call(bf16[16,384,128]{2,1,0:T(8,128)(2,1)} %all-to-all-done.refs_0_, bf16[16,256,128]{2,1,0:T(8,128)(2,1)S(1)} %all-to-all-done.1.refs_1_, f32[4096,128]{1,0:T(8,128)S(1)} %get-tuple-element.15.refs_2_, f32[1]{0:T(128)} %get-tuple-element.16.refs_3_), custom_call_target="tpu_custom_call" | custom-call | flops 17179869184 | bytes 8388608 | tf_op jit(solution)/shard_map/attend_other/pallas_call | solution.py:287
  97.7 15.4 %all_to_all.15.a_ref = bf16[16,128,128]{2,1,0:T(8,128)(2,1)S(1)} all-to-all(bf16[16,128,128]{2,1,0:T(8,128)(2,1)S(1)} %attend_other.1), channel_id=1, replica_groups=mesh['var'=8,'tm'=16] {'tm'}, dimensions={0} | all-to-all | bytes 1048576 | tf_op jit(solution)/shard_map/all_to_all | solution.py:22
  113.1 2.3 %project_out.1 = bf16[128,2,1024]{2,1,0:T(2,128)(2,1)} custom-call(bf16[16,128,128]{2,1,0:T(8,128)(2,1)S(1)} %all_to_all.15.a_ref, bf16[1024,1024]{1,0:T(8,128)(2,1)S(1)} %copy-done.2), custom_call_target="tpu_custom_call" | custom-call | flops 536870912 | bytes 2097152 | tf_op jit(solution)/shard_map/project_out/pallas_call | solution.py:321
  (12 shorter events, 0.0 us)
Async XLA Ops:
  0.0 25.6 %collective-permute-start.2 = (bf16[128,2,1024]{2,1,0:T(2,128)(2,1)}, bf16[128,2,1024]{2,1,0:T(2,128)(2,1)S(1)}, u32[]{:S(2)}, u32[]{:S(2)}) collective-permute-start(bf16[128,2,1024]{2,1,0:T(2,128)(2,1)} %refs_0_.1), channel_id=1, source_target_pairs={{0,96},{16,112},{32,0},{48,16},{64,32},{80,48},{96,64},{112,80},{1... | collective-permute-start | bytes 1572872 | tf_op jit(solution)/shard_map/ppermute | solution.py:355
  3.6 22.0 %collective-permute-start.1 = (bf16[128,2,1024]{2,1,0:T(2,128)(2,1)}, bf16[128,2,1024]{2,1,0:T(2,128)(2,1)S(1)}, u32[]{:S(2)}, u32[]{:S(2)}) collective-permute-start(bf16[128,2,1024]{2,1,0:T(2,128)(2,1)} %refs_0_.1), channel_id=1, source_target_pairs={{0,64},{16,80},{32,96},{48,112},{64,0},{80,16},{96,32},{112,48},{1... | collective-permute-start | bytes 1572872 | tf_op jit(solution)/shard_map/ppermute | solution.py:355
  3.9 26.6 %collective-permute-start = (bf16[128,2,1024]{2,1,0:T(2,128)(2,1)}, bf16[128,2,1024]{2,1,0:T(2,128)(2,1)S(1)}, u32[]{:S(2)}, u32[]{:S(2)}) collective-permute-start(bf16[128,2,1024]{2,1,0:T(2,128)(2,1)} %refs_0_.1), channel_id=1, source_target_pairs={{0,32},{16,48},{32,64},{48,80},{64,96},{80,112},{96,0},{112,16},{1... | collective-permute-start | bytes 1572872 | tf_op jit(solution)/shard_map/ppermute | solution.py:355
  10.5 20.8 %copy-start.4 = (bf16[128,2,1024]{2,1,0:T(2,128)(2,1)S(1)}, bf16[128,2,1024]{2,1,0:T(2,128)(2,1)}, u32[]{:S(2)}) copy-start(bf16[128,2,1024]{2,1,0:T(2,128)(2,1)} %refs_0_.1) | copy-start | bytes 1572868
  10.5 28.9 %all-to-all-start = ((bf16[16,384,128]{2,1,0:T(8,128)(2,1)}), bf16[16,384,128]{2,1,0:T(8,128)(2,1)}, u32[]{:S(2)}, u32[]{:S(2)}) async-start(bf16[16,384,128]{2,1,0:T(8,128)(2,1)} %project_own.1), calls=%async_computation | async-start | bytes 3145728 | tf_op jit(solution)/shard_map/all_to_all | solution.py:22
  25.6 4.9 %copy-start.5 = (bf16[128,2,1024]{2,1,0:T(2,128)(2,1)}, bf16[128,2,1024]{2,1,0:T(2,128)(2,1)S(1)}, u32[]{:S(2)}) copy-start(bf16[128,2,1024]{2,1,0:T(2,128)(2,1)S(1)} %collective-permute-done.1) | copy-start | bytes 1572868
  30.5 0.8 copy-start.6
  32.2 2.4 %copy-start = (bf16[1024,1024]{1,0:T(8,128)(2,1)S(1)}, bf16[1024,1024]{1,0:T(8,128)(2,1)}, u32[]{:S(2)}) copy-start(bf16[1024,1024]{1,0:T(8,128)(2,1)} %refs_2_.3) | copy-start | bytes 6291460
  32.2 2.4 %copy-start.3 = (f32[1024]{0:T(1024)S(1)}, f32[1024]{0:T(1024)}, u32[]{:S(2)}) copy-start(f32[1024]{0:T(1024)} %param.8) | copy-start | bytes 12292
  32.2 2.3 %collective-permute-start.3 = (bf16[128,2,1024]{2,1,0:T(2,128)(2,1)}, bf16[128,2,1024]{2,1,0:T(2,128)(2,1)}, u32[]{:S(2)}, u32[]{:S(2)}) collective-permute-start(bf16[128,2,1024]{2,1,0:T(2,128)(2,1)} %bitcast.9), channel_id=1, source_target_pairs={{0,16},{16,0},{32,48},{48,32},{64,80},{80,64},{96,112},{112,96},{1... | collective-permute-start | bytes 1572872 | tf_op jit(solution)/shard_map/ppermute | solution.py:367
  34.6 1.6 %copy-start.1 = (bf16[1024,1024]{1,0:T(8,128)(2,1)S(1)}, bf16[1024,1024]{1,0:T(8,128)(2,1)}, u32[]{:S(2)}) copy-start(bf16[1024,1024]{1,0:T(8,128)(2,1)} %refs_3_.3) | copy-start | bytes 6291460
  39.4 32.5 %all-to-all-start.1 = ((bf16[16,256,128]{2,1,0:T(8,128)(2,1)}), bf16[16,256,128]{2,1,0:T(8,128)(2,1)S(1)}, u32[]{:S(2)}, u32[]{:S(2)}) async-start(bf16[16,256,128]{2,1,0:T(8,128)(2,1)} %project_other.1), calls=%async_computation.1 | async-start | bytes 2097152 | tf_op jit(solution)/shard_map/all_to_all | solution.py:22
  71.9 41.3 %copy-start.2 = (bf16[1024,1024]{1,0:T(8,128)(2,1)S(1)}, bf16[1024,1024]{1,0:T(8,128)(2,1)}, u32[]{:S(2)}) copy-start(bf16[1024,1024]{1,0:T(8,128)(2,1)} %w_ref.1) | copy-start | bytes 6291460

commit v4 on v3

--- a/solution.py
+++ b/solution.py
@@ -118,7 +118,7 @@
     def at(tile, count=1):
         return pl.ds(pl.multiple_of(tile * TILE, TILE), count * TILE)
 
-    def prepare_queries(t, carry):
+    def prepare_queries(t):
         x = q_ref[t, (0 if final else rows) :].astype(jnp.float32)
         if not final:
             query_len[...] = jnp.maximum(query_len[...], lengths(x, same_half))
@@ -130,9 +130,8 @@
             later = jnp.where((lane > step) & (lane < base + 2 * per), LOW, jnp.float32(0.0))
             to = pl.ds(pl.multiple_of(t * rows + part * half, half), half)
             query[to] = jnp.where(low, y, later).astype(jnp.bfloat16)
-        return carry
-
-    def prepare(t, carry):
+
+    def prepare(t):
         block = pl.ds(pl.multiple_of(t * rows, rows), rows)
         kv = kv_ref[t, :rows].astype(jnp.float32)
         key_len[...] = jnp.maximum(key_len[...], lengths(kv, key_half))
@@ -143,18 +142,17 @@
         key[0, block] = jnp.where(low, kv, 0.0).astype(jnp.bfloat16)
         key[1, block] = jnp.where(low, kv, is_step).astype(jnp.bfloat16)
         value[block] = jnp.where(low, 1.0, kv).astype(jnp.bfloat16)
-        acc[block] = state_in[block] if final else jnp.zeros((rows, LANES), jnp.float32)
-        return carry
 
     query_len[...] = jnp.zeros_like(query_len)
     key_len[...] = jnp.zeros_like(key_len)
+    for t in range(HEADS):
+        prepare(t)
+        if not final:
+            prepare_queries(t)
     if final:
-        lax.fori_loop(0, HEADS, prepare, 0, unroll=8)
         fetch.wait()
-        lax.fori_loop(0, HEADS, prepare_queries, 0, unroll=8)
-    else:
-        both = lambda t, carry: prepare(t, prepare_queries(t, carry))
-        lax.fori_loop(0, HEADS, both, 0, unroll=8)
+        for t in range(HEADS):
+            prepare_queries(t)
     longest = longest_in[0] if final else jnp.max(query_len[...])
     fits = longest * jnp.max(key_len[...]) <= SAFE * SAFE
     if final:
@@ -171,6 +169,14 @@
 
     def weighted(p, v):
         return jnp.dot(p, v, preferred_element_type=jnp.float32)
+
+    def finish(t):
+        x = acc[t * rows : t * rows + half]
+        y = acc[t * rows + half : (t + 1) * rows]
+        low = low_lanes(x.shape)
+        num = jnp.where(low, swap(x), y)
+        den = jnp.where(low, x, swap(y))
+        out_ref[t] = (num / den).astype(jnp.bfloat16)
 
     @pl.when(fits)
     def _():
@@ -195,7 +201,12 @@
             for at_row, row, count, column, width in spans(first, j):
                 here = slice(at_row * rows, (at_row + count) * rows)
                 v = value[block_at(column, width)]
-                acc[block_at(row, count)] += weighted(p[here, : width * rows], v)
+                to = block_at(row, count)
+                part = weighted(p[here, : width * rows], v)
+                if j > 0:
+                    acc[to] += part
+                else:
+                    acc[to] = state_in[to] + part if final else part
 
         todo = [(first, j) for first in range(0, tiles, 2) for j in range(first + 2)]
         slots = (p0, p1)
@@ -204,9 +215,13 @@
             if n + 1 < len(todo):
                 weights(slots[(n + 1) % 2], *todo[n + 1])
             gather(slots[n % 2], *here)
+            if final and here[1] == here[0] + 1:
+                for t in range(here[0] * per, (here[0] + 2) * per):
+                    finish(t)
 
     @pl.when(jnp.logical_not(fits))
     def _():
+        acc[...] = state_in[...] if final else jnp.zeros_like(acc)
         lane = lax.broadcasted_iota(jnp.int32, (TILE, LANES), 1)
 
         def spread(x, n):
@@ -237,20 +252,9 @@
             return carry
 
         lax.fori_loop(0, tiles, row_block, 0)
-
-    if final:
-
-        def finish(t, carry):
-            base = pl.multiple_of(t * rows, rows)
-            x = acc[pl.ds(base, half)]
-            y = acc[pl.ds(base + half, half)]
-            low = low_lanes(x.shape)
-            num = jnp.where(low, swap(x), y)
-            den = jnp.where(low, x, swap(y))
-            out_ref[t] = (num / den).astype(jnp.bfloat16)
-            return carry
-
-        lax.fori_loop(0, HEADS, finish, 0, unroll=8)
+        if final:
+            for t in range(HEADS):
+                finish(t)
 
 
 def attend(*operands):

time: 118 us -> 115 us (0.975)
  the two profiles are of different devices: /device:TPU:1 before, /device:TPU:24 now
where the time goes in v4:
time: 115 us; the launch traced here: 114 us
  Pallas kernels  50 us (43%)
  blocking collectives  24.2 us (21%)
  starting transfers between devices  15.9 us (14%)
  waiting for transfers between devices  14.9 us (13%)
  other arithmetic  3.57 us (3%)
  between operations  2.89 us (3%)
  local copies, waits for them, and re-layouts  2.39 us (2%)
    pallas_call x2, Pallas kernels, attend(): pl.pallas_call(functools.partial(attend_kernel, final), in_specs=[far, wh...  38.6 us
    all_to_all x1, blocking collectives, exchange(): return lax.all_to_all(x, 'tm', split_axis=0, concat_axis=0, tiled=True)  24.2 us
    all_to_all x2, starting transfers between devices, exchange(): return lax.all_to_all(x, 'tm', split_axis=0, concat_axis=0, tiled=True)  12 us
    pallas_call x2, Pallas kernels, project(): pl.pallas_call(functools.partial(project_kernel, with_query), grid=(width...  9.05 us
    all_to_all x2, waiting for transfers between devices, exchange(): return lax.all_to_all(x, 'tm', split_axis=0, concat_axis=0, tiled=True)  7.82 us
    ppermute x3, waiting for transfers between devices, same_core(): held.append(lax.ppermute(x, 'var', pairs))  6.34 us
    ppermute x3, starting transfers between devices, same_core(): held.append(lax.ppermute(x, 'var', pairs))  3.87 us
    unnamed x14, local copies, waits for them, and re-layouts  2.39 us
  transfers between devices with their start and end apart: 6, of which 5 were waited for; matrix products, arithmetic and copies ran while one was open for 3% of the time, Pallas kernels for 19%

profile of v4, /device:TPU:24, one launch (start us, length us, event | category | flops | bytes accessed | tf_op | source)
XLA Modules:
  0.0 113.8 jit_solution(5114755662530396185)
XLA Ops:
  0.0 0.7 collective-permute-start.2
  0.7 0.9 collective-permute-start.1
  1.6 2.3 %collective-permute-start = (bf16[128,2,1024]{2,1,0:T(2,128)(2,1)}, bf16[128,2,1024]{2,1,0:T(2,128)(2,1)S(1)}, u32[]{:S(2)}, u32[]{:S(2)}) collective-permute-start(bf16[128,2,1024]{2,1,0:T(2,128)(2,1)} %refs_0_.1), channel_id=1, source_target_pairs={{0,32},{16,48},{32,64},{48,80},{64,96},{80,112},{96,0},{112,16},{1... | collective-permute-start | bytes 1572872 | tf_op jit(solution)/shard_map/ppermute | solution.py:359
  3.9 5.9 %project_own.1 = bf16[16,384,128]{2,1,0:T(8,128)(2,1)} custom-call(bf16[128,2,1024]{2,1,0:T(2,128)(2,1)} %refs_0_.1, f32[1,1024]{1,0:T(1,128)} %bitcast.17, bf16[1024,1024]{1,0:T(8,128)(2,1)} %refs_2_.3, bf16[1024,1024]{1,0:T(8,128)(2,1)} %refs_3_.3, bf16[1024,1024]{1,0:T(8,128)(2,1)} %refs_4_.1), custom_call_target="tpu_custom_call" | custom-call | flops 1610612736 | bytes 7340032 | tf_op jit(solution)/shard_map/project_own/pallas_call | solution.py:76
  9.7 8.1 %all-to-all-start = ((bf16[16,384,128]{2,1,0:T(8,128)(2,1)}), bf16[16,384,128]{2,1,0:T(8,128)(2,1)}, u32[]{:S(2)}, u32[]{:S(2)}) async-start(bf16[16,384,128]{2,1,0:T(8,128)(2,1)} %project_own.1), calls=%async_computation | async-start | bytes 3145728 | tf_op jit(solution)/shard_map/all_to_all | solution.py:22
  17.8 0.8 compare_select_fusion
  18.6 0.7 fusion
  20.6 5.7 %collective-permute-done.2 = bf16[128,2,1024]{2,1,0:T(2,128)(2,1)S(1)} collective-permute-done((bf16[128,2,1024]{2,1,0:T(2,128)(2,1)}, bf16[128,2,1024]{2,1,0:T(2,128)(2,1)S(1)}, u32[]{:S(2)}, u32[]{:S(2)}) %collective-permute-start.2) | collective-permute-done | bytes 524320 | tf_op jit(solution)/shard_map/ppermute | solution.py:359
  26.3 0.6 collective-permute-done
  26.9 0.2 copy-done.5
  27.1 0.6 copy-done.6
  27.7 0.9 broadcast_select_fusion.2
  30.2 0.7 collective-permute-done.3
  30.9 1.2 %broadcast_select_fusion.6 = bf16[32,8,1024]{2,1,0:T(8,128)(2,1)S(1)} fusion(bf16[32,8,1024]{2,1,0:T(8,128)(2,1)S(1)} %bitcast.22, pred[]{:T(512)S(6)} %eq.30, bf16[32,8,1024]{2,1,0:T(8,128)(2,1)} %bitcast.24, pred[]{:T(512)S(6)} %eq.31, bf16[32,8,1024]{2,1,0:T(8,128)(2,1)} %bitcast.26, pred[]{:T(512)S(6)} %eq.32, bf16[32,8,1024]{2,1,0:T(8,128)(2,1)S(1)} %bitcast.20, ...), kind=kLoop, calls=%fused_computation.6 | loop fusion | flops 1048576 | bytes 3145732 | tf_op jit(solution)/shard_map/jit(_where)/select_n | solution.py:348
  32.1 0.0 copy-start.1
  32.1 1.6 %copy-done.1 = bf16[1024,1024]{1,0:T(8,128)(2,1)S(1)} copy-done((bf16[1024,1024]{1,0:T(8,128)(2,1)S(1)}, bf16[1024,1024]{1,0:T(8,128)(2,1)}, u32[]{:S(2)}) %copy-start.1) | copy-done | bytes 2097176
  33.7 3.2 %project_other.1 = bf16[16,256,128]{2,1,0:T(8,128)(2,1)} custom-call(bf16[128,2,1024]{2,1,0:T(2,128)(2,1)S(1)} %bitcast.16, f32[1,1024]{1,0:T(1,128)S(1)} %bitcast.18, bf16[1024,1024]{1,0:T(8,128)(2,1)S(1)} %copy-done, bf16[1024,1024]{1,0:T(8,128)(2,1)S(1)} %copy-done.1), custom_call_target="tpu_custom_call" | custom-call | flops 1073741824 | bytes 5242880 | tf_op jit(solution)/shard_map/project_other/pallas_call | solution.py:76
  36.9 3.9 %all-to-all-done.refs_0_ = bf16[16,384,128]{2,1,0:T(8,128)(2,1)} async-done(((bf16[16,384,128]{2,1,0:T(8,128)(2,1)}), bf16[16,384,128]{2,1,0:T(8,128)(2,1)}, u32[]{:S(2)}, u32[]{:S(2)}) %all-to-all-start) | async-done | bytes 1572896 | tf_op jit(solution)/shard_map/all_to_all | solution.py:22
  40.8 3.9 %all-to-all-start.1 = ((bf16[16,256,128]{2,1,0:T(8,128)(2,1)}), bf16[16,256,128]{2,1,0:T(8,128)(2,1)S(1)}, u32[]{:S(2)}, u32[]{:S(2)}) async-start(bf16[16,256,128]{2,1,0:T(8,128)(2,1)} %project_other.1), calls=%async_computation.1 | async-start | bytes 2097152 | tf_op jit(solution)/shard_map/all_to_all | solution.py:22
  44.7 12.7 %attend_own.1 = (f32[4096,128]{1,0:T(8,128)S(1)}, f32[1]{0:T(128)}) custom-call(bf16[16,384,128]{2,1,0:T(8,128)(2,1)} %all-to-all-done.refs_0_), custom_call_target="tpu_custom_call" | custom-call | flops 17179869184 | bytes 8388608 | tf_op jit(solution)/shard_map/attend_own/pallas_call | solution.py:291
  57.4 3.9 %all-to-all-done.1.refs_1_ = bf16[16,256,128]{2,1,0:T(8,128)(2,1)S(1)} async-done(((bf16[16,256,128]{2,1,0:T(8,128)(2,1)}), bf16[16,256,128]{2,1,0:T(8,128)(2,1)S(1)}, u32[]{:S(2)}, u32[]{:S(2)}) %all-to-all-start.1) | async-done | bytes 1048608 | tf_op jit(solution)/shard_map/all_to_all | solution.py:22
  61.3 25.9 %attend_other.1 = bf16[16,128,128]{2,1,0:T(8,128)(2,1)S(1)} custom-call(bf16[16,384,128]{2,1,0:T(8,128)(2,1)} %all-to-all-done.refs_0_, bf16[16,256,128]{2,1,0:T(8,128)(2,1)S(1)} %all-to-all-done.1.refs_1_, f32[4096,128]{1,0:T(8,128)S(1)} %get-tuple-element.15.refs_2_, f32[1]{0:T(128)} %get-tuple-element.16.refs_3_), custom_call_target="tpu_custom_call" | custom-call | flops 17179869184 | bytes 8388608 | tf_op jit(solution)/shard_map/attend_other/pallas_call | solution.py:291
  87.3 24.2 %all_to_all.15.a_ref = bf16[16,128,128]{2,1,0:T(8,128)(2,1)S(1)} all-to-all(bf16[16,128,128]{2,1,0:T(8,128)(2,1)S(1)} %attend_other.1), channel_id=1, replica_groups=mesh['var'=8,'tm'=16] {'tm'}, dimensions={0} | all-to-all | bytes 1048576 | tf_op jit(solution)/shard_map/all_to_all | solution.py:22
  111.5 2.3 %project_out.1 = bf16[128,2,1024]{2,1,0:T(2,128)(2,1)} custom-call(bf16[16,128,128]{2,1,0:T(8,128)(2,1)S(1)} %all_to_all.15.a_ref, bf16[1024,1024]{1,0:T(8,128)(2,1)S(1)} %copy-done.2), custom_call_target="tpu_custom_call" | custom-call | flops 536870912 | bytes 2097152 | tf_op jit(solution)/shard_map/project_out/pallas_call | solution.py:325
  (12 shorter events, 0.0 us)
Async XLA Ops:
  0.0 26.3 %collective-permute-start.2 = (bf16[128,2,1024]{2,1,0:T(2,128)(2,1)}, bf16[128,2,1024]{2,1,0:T(2,128)(2,1)S(1)}, u32[]{:S(2)}, u32[]{:S(2)}) collective-permute-start(bf16[128,2,1024]{2,1,0:T(2,128)(2,1)} %refs_0_.1), channel_id=1, source_target_pairs={{0,96},{16,112},{32,0},{48,16},{64,32},{80,48},{96,64},{112,80},{1... | collective-permute-start | bytes 1572872 | tf_op jit(solution)/shard_map/ppermute | solution.py:359
  0.7 25.6 %collective-permute-start.1 = (bf16[128,2,1024]{2,1,0:T(2,128)(2,1)}, bf16[128,2,1024]{2,1,0:T(2,128)(2,1)S(1)}, u32[]{:S(2)}, u32[]{:S(2)}) collective-permute-start(bf16[128,2,1024]{2,1,0:T(2,128)(2,1)} %refs_0_.1), channel_id=1, source_target_pairs={{0,64},{16,80},{32,96},{48,112},{64,0},{80,16},{96,32},{112,48},{1... | collective-permute-start | bytes 1572872 | tf_op jit(solution)/shard_map/ppermute | solution.py:359
  1.6 25.3 %collective-permute-start = (bf16[128,2,1024]{2,1,0:T(2,128)(2,1)}, bf16[128,2,1024]{2,1,0:T(2,128)(2,1)S(1)}, u32[]{:S(2)}, u32[]{:S(2)}) collective-permute-start(bf16[128,2,1024]{2,1,0:T(2,128)(2,1)} %refs_0_.1), channel_id=1, source_target_pairs={{0,32},{16,48},{32,64},{48,80},{64,96},{80,112},{96,0},{112,16},{1... | collective-permute-start | bytes 1572872 | tf_op jit(solution)/shard_map/ppermute | solution.py:359
  9.7 18.0 %copy-start.4 = (bf16[128,2,1024]{2,1,0:T(2,128)(2,1)S(1)}, bf16[128,2,1024]{2,1,0:T(2,128)(2,1)}, u32[]{:S(2)}) copy-start(bf16[128,2,1024]{2,1,0:T(2,128)(2,1)} %refs_0_.1) | copy-start | bytes 1572868
  9.7 31.1 %all-to-all-start = ((bf16[16,384,128]{2,1,0:T(8,128)(2,1)}), bf16[16,384,128]{2,1,0:T(8,128)(2,1)}, u32[]{:S(2)}, u32[]{:S(2)}) async-start(bf16[16,384,128]{2,1,0:T(8,128)(2,1)} %project_own.1), calls=%async_computation | async-start | bytes 3145728 | tf_op jit(solution)/shard_map/all_to_all | solution.py:22
  26.3 0.8 copy-start.5
  26.9 0.8 copy-start.6
  28.6 3.4 %copy-start = (bf16[1024,1024]{1,0:T(8,128)(2,1)S(1)}, bf16[1024,1024]{1,0:T(8,128)(2,1)}, u32[]{:S(2)}) copy-start(bf16[1024,1024]{1,0:T(8,128)(2,1)} %refs_2_.3) | copy-start | bytes 6291460
  28.6 3.4 %copy-start.3 = (f32[1024]{0:T(1024)S(1)}, f32[1024]{0:T(1024)}, u32[]{:S(2)}) copy-start(f32[1024]{0:T(1024)} %param.8) | copy-start | bytes 12292
  28.6 2.3 %collective-permute-start.3 = (bf16[128,2,1024]{2,1,0:T(2,128)(2,1)}, bf16[128,2,1024]{2,1,0:T(2,128)(2,1)}, u32[]{:S(2)}, u32[]{:S(2)}) collective-permute-start(bf16[128,2,1024]{2,1,0:T(2,128)(2,1)} %bitcast.9), channel_id=1, source_target_pairs={{0,16},{16,0},{32,48},{48,32},{64,80},{80,64},{96,112},{112,96},{1... | collective-permute-start | bytes 1572872 | tf_op jit(solution)/shard_map/ppermute | solution.py:371
  32.1 1.6 %copy-start.1 = (bf16[1024,1024]{1,0:T(8,128)(2,1)S(1)}, bf16[1024,1024]{1,0:T(8,128)(2,1)}, u32[]{:S(2)}) copy-start(bf16[1024,1024]{1,0:T(8,128)(2,1)} %refs_3_.3) | copy-start | bytes 6291460
  40.8 20.5 %all-to-all-start.1 = ((bf16[16,256,128]{2,1,0:T(8,128)(2,1)}), bf16[16,256,128]{2,1,0:T(8,128)(2,1)S(1)}, u32[]{:S(2)}, u32[]{:S(2)}) async-start(bf16[16,256,128]{2,1,0:T(8,128)(2,1)} %project_other.1), calls=%async_computation.1 | async-start | bytes 2097152 | tf_op jit(solution)/shard_map/all_to_all | solution.py:22
  61.3 50.2 %copy-start.2 = (bf16[1024,1024]{1,0:T(8,128)(2,1)S(1)}, bf16[1024,1024]{1,0:T(8,128)(2,1)}, u32[]{:S(2)}) copy-start(bf16[1024,1024]{1,0:T(8,128)(2,1)} %w_ref.1) | copy-start | bytes 6291460

commit v5 on v4

--- a/solution.py
+++ b/solution.py
@@ -90,6 +90,39 @@
             transcendentals=0,
         ),
         name="project_own" if with_query else "project_other",
+    )(x, gain, *weights)
+
+
+def other_kernel(x_ref, gain_ref, wk_ref, wv_ref, out_ref):
+    normed = normed_rows(x_ref, gain_ref)
+    for c in range(0, wk_ref.shape[1], COLS):
+        cols = slice(c, c + COLS)
+        k = jnp.dot(normed, wk_ref[:, cols], preferred_element_type=jnp.float32)
+        v = jnp.dot(normed, wv_ref[:, cols], preferred_element_type=jnp.float32)
+        for p in range(COLS // LANES):
+            head = c // HEAD + 2 * p
+            kt, vt = k[:, p * LANES : (p + 1) * LANES], v[:, p * LANES : (p + 1) * LANES]
+            low = low_lanes(kt.shape)
+            out_ref[head] = jnp.where(low, kt, swap(vt)).astype(jnp.bfloat16)
+            out_ref[head + 1] = jnp.where(low, swap(kt), vt).astype(jnp.bfloat16)
+
+
+def project_other(x, gain, weights):
+    var_rows, step_rows, width = x.shape
+    rows = var_rows * step_rows
+    whole = pl.BlockSpec(memory_space=pltpu.VMEM)
+    return pl.pallas_call(
+        other_kernel,
+        in_specs=[whole] * 4,
+        out_specs=whole,
+        out_shape=jax.ShapeDtypeStruct((HEADS, rows, LANES), jnp.bfloat16),
+        compiler_params=pltpu.CompilerParams(vmem_limit_bytes=20 << 20),
+        cost_estimate=pl.CostEstimate(
+            flops=4 * rows * width * width,
+            bytes_accessed=4 * width * width + 4 * rows * width,
+            transcendentals=0,
+        ),
+        name="project_other",
     )(x, gain, *weights)
 
 
@@ -379,7 +412,7 @@
     packed = project(tokens, gain, (w_key, w_value, w_query))
     *held, _ = lax.optimization_barrier((*held, packed))
     x_other = pick_other([tokens, *held], adjacency)
-    kv_other = project(x_other, gain, (w_key, w_value))
+    kv_other = project_other(x_other, gain, (w_key, w_value))
     packed, _ = lax.optimization_barrier((exchange(packed), kv_other))
     kv_other = exchange(kv_other)
     att = exchange(attend(packed, kv_other, *attend(packed)))

time: 115 us -> 116 us (level)
  the two profiles are of different devices: /device:TPU:24 before, /device:TPU:8 now
where the time goes in v5:
time: 116 us; the launch traced here: 115 us
  Pallas kernels  61.2 us (53%)
  blocking collectives  17.1 us (15%)
  starting transfers between devices  16.6 us (14%)
  waiting for transfers between devices  12.5 us (11%)
  between operations  2.91 us (3%)
  other arithmetic  2.53 us (2%)
  local copies, waits for them, and re-layouts  2.4 us (2%)
    pallas_call x2, Pallas kernels, attend(): pl.pallas_call(functools.partial(attend_kernel, final), in_specs=[far, wh...  50.3 us
    all_to_all x1, blocking collectives, exchange(): return lax.all_to_all(x, 'tm', split_axis=0, concat_axis=0, tiled=True)  17.1 us
    all_to_all x2, starting transfers between devices, exchange(): return lax.all_to_all(x, 'tm', split_axis=0, concat_axis=0, tiled=True)  11.7 us
    all_to_all x2, waiting for transfers between devices, exchange(): return lax.all_to_all(x, 'tm', split_axis=0, concat_axis=0, tiled=True)  6.49 us
    pallas_call x1, Pallas kernels, project(): pl.pallas_call(functools.partial(project_kernel, with_query), grid=(width...  5.86 us
    ppermute x3, waiting for transfers between devices, same_core(): held.append(lax.ppermute(x, 'var', pairs))  5.28 us
    ppermute x3, starting transfers between devices, same_core(): held.append(lax.ppermute(x, 'var', pairs))  4.93 us
    pallas_call x1, Pallas kernels, project_other(): pl.pallas_call(other_kernel, in_specs=[whole] * 4, out_specs=whole, out_s...  2.74 us
  transfers between devices with their start and end apart: 6, of which 4 were waited for; matrix products, arithmetic and copies ran while one was open for 2% of the time, Pallas kernels for 29%

profile of v5, /device:TPU:8, one launch (start us, length us, event | category | flops | bytes accessed | tf_op | source)
XLA Modules:
  0.0 115.2 jit_solution(9201933063432740416)
XLA Ops:
  0.0 0.4 collective-permute-start.2
  0.4 2.7 %collective-permute-start.1 = (bf16[128,2,1024]{2,1,0:T(2,128)(2,1)}, bf16[128,2,1024]{2,1,0:T(2,128)(2,1)S(1)}, u32[]{:S(2)}, u32[]{:S(2)}) collective-permute-start(bf16[128,2,1024]{2,1,0:T(2,128)(2,1)} %refs_0_.1), channel_id=1, source_target_pairs={{0,64},{16,80},{32,96},{48,112},{64,0},{80,16},{96,32},{112,48},{1... | collective-permute-start | bytes 1572872 | tf_op jit(solution)/shard_map/ppermute | solution.py:392
  3.0 1.9 %collective-permute-start = (bf16[128,2,1024]{2,1,0:T(2,128)(2,1)}, bf16[128,2,1024]{2,1,0:T(2,128)(2,1)S(1)}, u32[]{:S(2)}, u32[]{:S(2)}) collective-permute-start(bf16[128,2,1024]{2,1,0:T(2,128)(2,1)} %refs_0_.1), channel_id=1, source_target_pairs={{0,32},{16,48},{32,64},{48,80},{64,96},{80,112},{96,0},{112,16},{1... | collective-permute-start | bytes 1572872 | tf_op jit(solution)/shard_map/ppermute | solution.py:392
  4.9 5.9 %project_own.1 = bf16[16,384,128]{2,1,0:T(8,128)(2,1)} custom-call(bf16[128,2,1024]{2,1,0:T(2,128)(2,1)} %refs_0_.1, f32[1,1024]{1,0:T(1,128)} %bitcast.17, bf16[1024,1024]{1,0:T(8,128)(2,1)} %wk_ref.1, bf16[1024,1024]{1,0:T(8,128)(2,1)} %wv_ref.1, bf16[1024,1024]{1,0:T(8,128)(2,1)} %refs_4_.1), custom_call_target="tpu_custom_call" | custom-call | flops 1610612736 | bytes 7340032 | tf_op jit(solution)/shard_map/project_own/pallas_call | solution.py:76
  10.8 8.1 %all-to-all-start = ((bf16[16,384,128]{2,1,0:T(8,128)(2,1)}), bf16[16,384,128]{2,1,0:T(8,128)(2,1)}, u32[]{:S(2)}, u32[]{:S(2)}) async-start(bf16[16,384,128]{2,1,0:T(8,128)(2,1)} %project_own.1), calls=%async_computation | async-start | bytes 3145728 | tf_op jit(solution)/shard_map/all_to_all | solution.py:22
  18.9 0.8 compare_select_fusion
  19.6 0.7 fusion
  21.7 0.0 collective-permute-done.2
  21.7 4.5 %collective-permute-done.1 = bf16[128,2,1024]{2,1,0:T(2,128)(2,1)S(1)} collective-permute-done((bf16[128,2,1024]{2,1,0:T(2,128)(2,1)}, bf16[128,2,1024]{2,1,0:T(2,128)(2,1)S(1)}, u32[]{:S(2)}, u32[]{:S(2)}) %collective-permute-start.1) | collective-permute-done | bytes 524320 | tf_op jit(solution)/shard_map/ppermute | solution.py:392
  26.1 0.8 collective-permute-done
  26.9 0.8 copy-done.6
  27.7 0.9 broadcast_select_fusion.2
  30.2 0.7 collective-permute-done.3
  30.9 0.1 broadcast_select_fusion.6
  31.0 0.0 copy-start.1
  31.0 1.6 %copy-done.1 = bf16[1024,1024]{1,0:T(8,128)(2,1)S(1)} copy-done((bf16[1024,1024]{1,0:T(8,128)(2,1)S(1)}, bf16[1024,1024]{1,0:T(8,128)(2,1)}, u32[]{:S(2)}) %copy-start.1) | copy-done | bytes 2097176
  32.6 2.7 %project_other.1 = bf16[16,256,128]{2,1,0:T(8,128)(2,1)} custom-call(bf16[128,2,1024]{2,1,0:T(2,128)(2,1)S(1)} %bitcast.16, f32[1,1024]{1,0:T(1,128)S(1)} %bitcast.18, bf16[1024,1024]{1,0:T(8,128)(2,1)S(1)} %copy-done, bf16[1024,1024]{1,0:T(8,128)(2,1)S(1)} %copy-done.1), custom_call_target="tpu_custom_call" | custom-call | flops 1073741824 | bytes 5242880 | tf_op jit(solution)/shard_map/project_other/pallas_call | solution.py:114
  35.4 6.5 %all-to-all-done.refs_0_ = bf16[16,384,128]{2,1,0:T(8,128)(2,1)} async-done(((bf16[16,384,128]{2,1,0:T(8,128)(2,1)}), bf16[16,384,128]{2,1,0:T(8,128)(2,1)}, u32[]{:S(2)}, u32[]{:S(2)}) %all-to-all-start) | async-done | bytes 1572896 | tf_op jit(solution)/shard_map/all_to_all | solution.py:22
  41.9 3.7 %all-to-all-start.1 = ((bf16[16,256,128]{2,1,0:T(8,128)(2,1)}), bf16[16,256,128]{2,1,0:T(8,128)(2,1)S(1)}, u32[]{:S(2)}, u32[]{:S(2)}) async-start(bf16[16,256,128]{2,1,0:T(8,128)(2,1)} %project_other.1), calls=%async_computation.1 | async-start | bytes 2097152 | tf_op jit(solution)/shard_map/all_to_all | solution.py:22
  45.5 24.3 %attend_own.1 = (f32[4096,128]{1,0:T(8,128)S(1)}, f32[1]{0:T(128)}) custom-call(bf16[16,384,128]{2,1,0:T(8,128)(2,1)} %all-to-all-done.refs_0_), custom_call_target="tpu_custom_call" | custom-call | flops 17179869184 | bytes 8388608 | tf_op jit(solution)/shard_map/attend_own/pallas_call | solution.py:324
  69.9 0.0 copy-start.2
  69.9 26.0 %attend_other.1 = bf16[16,128,128]{2,1,0:T(8,128)(2,1)S(1)} custom-call(bf16[16,384,128]{2,1,0:T(8,128)(2,1)} %all-to-all-done.refs_0_, bf16[16,256,128]{2,1,0:T(8,128)(2,1)S(1)} %all-to-all-done.1.refs_1_, f32[4096,128]{1,0:T(8,128)S(1)} %get-tuple-element.15.refs_2_, f32[1]{0:T(128)} %get-tuple-element.16.refs_3_), custom_call_target="tpu_custom_call" | custom-call | flops 17179869184 | bytes 8388608 | tf_op jit(solution)/shard_map/attend_other/pallas_call | solution.py:324
  95.8 17.1 %all_to_all.15.a_ref = bf16[16,128,128]{2,1,0:T(8,128)(2,1)S(1)} all-to-all(bf16[16,128,128]{2,1,0:T(8,128)(2,1)S(1)} %attend_other.1), channel_id=1, replica_groups=mesh['var'=8,'tm'=16] {'tm'}, dimensions={0} | all-to-all | bytes 1048576 | tf_op jit(solution)/shard_map/all_to_all | solution.py:22
  112.9 2.3 %project_out.1 = bf16[128,2,1024]{2,1,0:T(2,128)(2,1)} custom-call(bf16[16,128,128]{2,1,0:T(8,128)(2,1)S(1)} %all_to_all.15.a_ref, bf16[1024,1024]{1,0:T(8,128)(2,1)S(1)} %copy-done.2), custom_call_target="tpu_custom_call" | custom-call | flops 536870912 | bytes 2097152 | tf_op jit(solution)/shard_map/project_out/pallas_call | solution.py:358
  (12 shorter events, 0.0 us)
Async XLA Ops:
  0.0 21.7 %collective-permute-start.2 = (bf16[128,2,1024]{2,1,0:T(2,128)(2,1)}, bf16[128,2,1024]{2,1,0:T(2,128)(2,1)S(1)}, u32[]{:S(2)}, u32[]{:S(2)}) collective-permute-start(bf16[128,2,1024]{2,1,0:T(2,128)(2,1)} %refs_0_.1), channel_id=1, source_target_pairs={{0,96},{16,112},{32,0},{48,16},{64,32},{80,48},{96,64},{112,80},{1... | collective-permute-start | bytes 1572872 | tf_op jit(solution)/shard_map/ppermute | solution.py:392
  0.4 25.8 %collective-permute-start.1 = (bf16[128,2,1024]{2,1,0:T(2,128)(2,1)}, bf16[128,2,1024]{2,1,0:T(2,128)(2,1)S(1)}, u32[]{:S(2)}, u32[]{:S(2)}) collective-permute-start(bf16[128,2,1024]{2,1,0:T(2,128)(2,1)} %refs_0_.1), channel_id=1, source_target_pairs={{0,64},{16,80},{32,96},{48,112},{64,0},{80,16},{96,32},{112,48},{1... | collective-permute-start | bytes 1572872 | tf_op jit(solution)/shard_map/ppermute | solution.py:392
  3.0 23.9 %collective-permute-start = (bf16[128,2,1024]{2,1,0:T(2,128)(2,1)}, bf16[128,2,1024]{2,1,0:T(2,128)(2,1)S(1)}, u32[]{:S(2)}, u32[]{:S(2)}) collective-permute-start(bf16[128,2,1024]{2,1,0:T(2,128)(2,1)} %refs_0_.1), channel_id=1, source_target_pairs={{0,32},{16,48},{32,64},{48,80},{64,96},{80,112},{96,0},{112,16},{1... | collective-permute-start | bytes 1572872 | tf_op jit(solution)/shard_map/ppermute | solution.py:392
  10.8 16.9 %copy-start.4 = (bf16[128,2,1024]{2,1,0:T(2,128)(2,1)S(1)}, bf16[128,2,1024]{2,1,0:T(2,128)(2,1)}, u32[]{:S(2)}) copy-start(bf16[128,2,1024]{2,1,0:T(2,128)(2,1)} %refs_0_.1) | copy-start | bytes 1572868
  10.8 31.1 %all-to-all-start = ((bf16[16,384,128]{2,1,0:T(8,128)(2,1)}), bf16[16,384,128]{2,1,0:T(8,128)(2,1)}, u32[]{:S(2)}, u32[]{:S(2)}) async-start(bf16[16,384,128]{2,1,0:T(8,128)(2,1)} %project_own.1), calls=%async_computation | async-start | bytes 3145728 | tf_op jit(solution)/shard_map/all_to_all | solution.py:22
  26.1 0.8 copy-start.5
  26.9 0.8 copy-start.6
  28.6 2.4 %copy-start = (bf16[1024,1024]{1,0:T(8,128)(2,1)S(1)}, bf16[1024,1024]{1,0:T(8,128)(2,1)}, u32[]{:S(2)}) copy-start(bf16[1024,1024]{1,0:T(8,128)(2,1)} %wk_ref.1) | copy-start | bytes 6291460
  28.6 2.4 %copy-start.3 = (f32[1024]{0:T(1024)S(1)}, f32[1024]{0:T(1024)}, u32[]{:S(2)}) copy-start(f32[1024]{0:T(1024)} %param.8) | copy-start | bytes 12292
  28.6 2.3 %collective-permute-start.3 = (bf16[128,2,1024]{2,1,0:T(2,128)(2,1)}, bf16[128,2,1024]{2,1,0:T(2,128)(2,1)}, u32[]{:S(2)}, u32[]{:S(2)}) collective-permute-start(bf16[128,2,1024]{2,1,0:T(2,128)(2,1)} %bitcast.9), channel_id=1, source_target_pairs={{0,16},{16,0},{32,48},{48,32},{64,80},{80,64},{96,112},{112,96},{1... | collective-permute-start | bytes 1572872 | tf_op jit(solution)/shard_map/ppermute | solution.py:404
  31.0 1.6 %copy-start.1 = (bf16[1024,1024]{1,0:T(8,128)(2,1)S(1)}, bf16[1024,1024]{1,0:T(8,128)(2,1)}, u32[]{:S(2)}) copy-start(bf16[1024,1024]{1,0:T(8,128)(2,1)} %wv_ref.1) | copy-start | bytes 6291460
  41.9 28.0 %all-to-all-start.1 = ((bf16[16,256,128]{2,1,0:T(8,128)(2,1)}), bf16[16,256,128]{2,1,0:T(8,128)(2,1)S(1)}, u32[]{:S(2)}, u32[]{:S(2)}) async-start(bf16[16,256,128]{2,1,0:T(8,128)(2,1)} %project_other.1), calls=%async_computation.1 | async-start | bytes 2097152 | tf_op jit(solution)/shard_map/all_to_all | solution.py:22
  69.9 43.0 %copy-start.2 = (bf16[1024,1024]{1,0:T(8,128)(2,1)S(1)}, bf16[1024,1024]{1,0:T(8,128)(2,1)}, u32[]{:S(2)}) copy-start(bf16[1024,1024]{1,0:T(8,128)(2,1)} %w_ref.1) | copy-start | bytes 6291460
